TPU v7x, 32 devices: a whole 2x2x4 slice. The times are simulated.
32 devices in a mesh: dp: 4 (over x, core), fsdp: 8 (over z, y).
Axes of the slice: x: 2, y: 2, z: 4, core: 2. Of those that a mesh axis runs over, the one named last changes fastest.
Arguments:
- patches: bfloat16 [8, 16, 197, 768], P('fsdp', 'dp'), may hold values from -64 to 64
- counts: int32 [8], P('fsdp'), may hold values from 8 to 16, as said below
- captions: bfloat16 [32, 512], P(('dp', 'fsdp')), may hold values from -6 to 6
- matches: int32 [8], P('fsdp'), may hold values from 0 to 31
- courier: bfloat16 [768, 768], P('fsdp'), may hold values from -0.21875 to 0.21875
- courier_gain: bfloat16 [768], P('fsdp'), may hold values from 0.5 to 1.5
- courier_heads: bfloat16 [768, 2304], P('fsdp'), may hold values from -0.21875 to 0.21875
- courier_merge: bfloat16 [768, 768], P('fsdp'), may hold values from -0.4375 to 0.4375
- attend_gain: bfloat16 [768], P('fsdp'), may hold values from 0.5 to 1.5
- attend_heads: bfloat16 [768, 2304], P('fsdp'), may hold values from -0.21875 to 0.21875
- attend_merge: bfloat16 [768, 768], P('fsdp'), may hold values from -0.875 to 0.875
- expand_gain: bfloat16 [768], P('fsdp'), may hold values from 0.5 to 1.5
- expand_weight: bfloat16 [768, 3072], P('fsdp'), may hold values from -0.21875 to 0.21875
- shrink_weight: bfloat16 [3072, 768], P('fsdp'), may hold values from -0.109375 to 0.109375
- projection: bfloat16 [768, 512], P('fsdp'), may hold values from -0.21875 to 0.21875
Outputs:
- loss: float32 [8], P('fsdp')
- patch_gradient: bfloat16 [8, 16, 197, 768], P('fsdp', 'dp')
- courier_gradient: float32 [768, 768], P('fsdp')
- courier_gain_gradient: float32 [768], P('fsdp')
- courier_heads_gradient: float32 [768, 2304], P('fsdp')
- courier_merge_gradient: float32 [768, 768], P('fsdp')
- attend_gain_gradient: float32 [768], P('fsdp')
- attend_heads_gradient: float32 [768, 2304], P('fsdp')
- attend_merge_gradient: float32 [768, 768], P('fsdp')
- expand_gain_gradient: float32 [768], P('fsdp')
- expand_weight_gradient: float32 [768, 3072], P('fsdp')
- shrink_weight_gradient: float32 [3072, 768], P('fsdp')
- projection_gradient: float32 [768, 512], P('fsdp')
Inputs may be any that keep to these rules, and one draw needn't show every extreme that they name: `counts`: each video has 8 or 16 frames, and both occur in every draw.
All inputs are finite; a program needn't handle non-finite values.
Results may differ from a plain program's by a relative error of at most 0.018.
Values may be sent and summed in bfloat16 or wider, within the bound.
A program may use at most 192 MiB of HBM per device.

v0:
```python
import jax
import jax.numpy as jnp
from jax import lax
from jax.sharding import PartitionSpec as P

HEADS = 12
HEAD = 64
MICRO = 2


EPSILON = 1e-05
LOGIT_SCALE = 64.0


def joined_2(value, axis, join):
    pieces = jax.tree.map(lambda part: lax.all_gather(part, axis), value)
    head = jax.tree.map(lambda part: part[0], pieces)
    tail = jax.tree.map(lambda part: part[1:], pieces)
    running, _ = lax.scan(lambda running, share: (join(running, share), None), head, tail)
    return running


def layer_norm(value, gain):
    center = value - jnp.mean(value, -1, keepdims=True)
    spread = jnp.mean(center * center, -1, keepdims=True)
    return center * lax.rsqrt(spread + EPSILON) * gain


def norm_back(value, gain, upstream):
    _, pull = jax.vjp(layer_norm, value, gain)
    return pull(upstream)


def quick_gelu(value):
    return value * jax.nn.sigmoid(1.702 * value)


def unit_rows(value):
    return value * lax.rsqrt(jnp.sum(value * value, -1, keepdims=True) + 1e-06)


def split_heads(mixed, query_count):
    batch, length, triple = mixed.shape
    width = triple // 3
    rounded = mixed.astype(jnp.bfloat16)
    queries = rounded[:, :query_count, :width].reshape(batch, query_count, HEADS, HEAD)
    keys = rounded[:, :, width : 2 * width].reshape(batch, length, HEADS, HEAD)
    values = rounded[:, :, 2 * width :].reshape(batch, length, HEADS, HEAD)
    return (queries, keys, values)


def scores_of(queries, keys, key_mask):
    scores = jnp.einsum(
        "bqhd,bkhd->bhqk", queries, keys, preferred_element_type=jnp.float32
    ) * HEAD ** (-0.5)
    if key_mask is not None:
        scores = jnp.where(key_mask[:, None, None, :], scores, -1000000000.0)
    return scores


def attend_forward(queries, keys, values, key_mask):
    scores = scores_of(queries, keys, key_mask)
    peak = jnp.max(scores, -1, keepdims=True)
    raised = jnp.exp(scores - peak)
    total = jnp.sum(raised, -1, keepdims=True)
    shares = (raised / total).astype(jnp.bfloat16)
    joined = jnp.einsum("bhqk,bkhd->bqhd", shares, values, preferred_element_type=jnp.float32)
    batch, count = (joined.shape[0], joined.shape[1])
    return (
        joined.reshape(batch, count, HEADS * HEAD).astype(jnp.bfloat16),
        peak + jnp.log(total),
        shares,
    )


def attend_backward(queries, keys, values, key_mask, normalizer, shares, upstream):
    batch, count, width = upstream.shape
    upstream_low = upstream.astype(jnp.bfloat16).reshape(batch, count, HEADS, HEAD)
    chances = jnp.exp(scores_of(queries, keys, key_mask) - normalizer)
    share_grad = jnp.einsum(
        "bqhd,bkhd->bhqk", upstream_low, values, preferred_element_type=jnp.float32
    )
    value_grad = jnp.einsum(
        "bhqk,bqhd->bkhd", shares, upstream_low, preferred_element_type=jnp.float32
    )
    inner = jnp.sum(chances * share_grad, -1, keepdims=True)
    score_grad = (chances * (share_grad - inner)).astype(jnp.bfloat16)
    query_grad = jnp.einsum(
        "bhqk,bkhd->bqhd", score_grad, keys, preferred_element_type=jnp.float32
    ) * HEAD ** (-0.5)
    key_grad = jnp.einsum(
        "bhqk,bqhd->bkhd", score_grad, queries, preferred_element_type=jnp.float32
    ) * HEAD ** (-0.5)
    length = keys.shape[1]
    return (
        query_grad.reshape(batch, count, width),
        key_grad.reshape(batch, length, width),
        value_grad.reshape(batch, length, width),
    )


def frame_forward(block, message_rows, weights):
    attend_gain, attend_heads, attend_merge, expand_gain, expand_weight, shrink_weight = weights
    frames = block.astype(jnp.float32)
    tokens = jnp.concatenate([frames, message_rows[:, None, :]], 1)
    normed = layer_norm(tokens, attend_gain).astype(jnp.bfloat16)
    mixed = jnp.einsum("btd,de->bte", normed, attend_heads, preferred_element_type=jnp.float32)
    queries, keys, values = split_heads(mixed, block.shape[1])
    seen, normalizer, shares = attend_forward(queries, keys, values, None)
    hidden = frames + jnp.einsum(
        "bpd,de->bpe", seen, attend_merge, preferred_element_type=jnp.float32
    )
    normed_two = layer_norm(hidden, expand_gain).astype(jnp.bfloat16)
    grown = jnp.einsum("bpd,dm->bpm", normed_two, expand_weight, preferred_element_type=jnp.float32)
    gated = quick_gelu(grown).astype(jnp.bfloat16)
    result = hidden + jnp.einsum(
        "bpm,md->bpd", gated, shrink_weight, preferred_element_type=jnp.float32
    )
    kept = (
        tokens,
        normed,
        queries,
        keys,
        values,
        shares,
        normalizer,
        seen,
        hidden,
        normed_two,
        grown,
        gated,
    )
    return (jnp.sum(result, 1), kept)


def frame_backward(kept, upstream, weights):
    attend_gain, attend_heads, attend_merge, expand_gain, expand_weight, shrink_weight = weights
    (
        tokens,
        normed,
        queries,
        keys,
        values,
        shares,
        normalizer,
        seen,
        hidden,
        normed_two,
        grown,
        gated,
    ) = kept
    patch_count = hidden.shape[1]
    upstream_low = upstream.astype(jnp.bfloat16)
    shrink_grad = jnp.einsum("bpm,bd->md", gated, upstream_low, preferred_element_type=jnp.float32)
    gated_grad = jnp.einsum(
        "bd,md->bm", upstream_low, shrink_weight, preferred_element_type=jnp.float32
    )
    _, gelu_pull = jax.vjp(quick_gelu, grown)
    grown_grad = gelu_pull(jnp.broadcast_to(gated_grad[:, None, :], grown.shape))[0].astype(
        jnp.bfloat16
    )
    expand_grad = jnp.einsum(
        "bpd,bpm->dm", normed_two, grown_grad, preferred_element_type=jnp.float32
    )
    normed_two_grad = jnp.einsum(
        "bpm,dm->bpd", grown_grad, expand_weight, preferred_element_type=jnp.float32
    )
    hidden_grad, expand_gain_grad = norm_back(hidden, expand_gain, normed_two_grad)
    hidden_grad = hidden_grad + upstream[:, None, :]
    hidden_low = hidden_grad.astype(jnp.bfloat16)
    merge_grad = jnp.einsum("bpd,bpe->de", seen, hidden_low, preferred_element_type=jnp.float32)
    seen_grad = jnp.einsum(
        "bpe,de->bpd", hidden_low, attend_merge, preferred_element_type=jnp.float32
    )
    query_grad, key_grad, value_grad = attend_backward(
        queries, keys, values, None, normalizer, shares, seen_grad
    )
    length = tokens.shape[1]
    query_grad = jnp.pad(query_grad, ((0, 0), (0, length - patch_count), (0, 0)))
    mixed_grad = jnp.concatenate([query_grad, key_grad, value_grad], 2).astype(jnp.bfloat16)
    heads_grad = jnp.einsum("btd,bte->de", normed, mixed_grad, preferred_element_type=jnp.float32)
    normed_grad = jnp.einsum(
        "bte,de->btd", mixed_grad, attend_heads, preferred_element_type=jnp.float32
    )
    token_grad, attend_gain_grad = norm_back(tokens, attend_gain, normed_grad)
    patch_grad = hidden_grad + token_grad[:, :patch_count]
    block_grads = (
        attend_gain_grad,
        heads_grad,
        merge_grad,
        expand_gain_grad,
        expand_grad,
        shrink_grad,
    )
    return (patch_grad, token_grad[:, patch_count], block_grads)


def shards(
    patches,
    counts,
    captions,
    matches,
    courier,
    courier_gain,
    courier_heads,
    courier_merge,
    attend_gain,
    attend_heads,
    attend_merge,
    expand_gain,
    expand_weight,
    shrink_weight,
    projection,
):
    videos, local_frames, patch_count, width = patches.shape
    frame_total = local_frames * lax.axis_size("dp")
    offset = lax.axis_index("dp") * local_frames
    rows = videos * local_frames
    per_block = rows // MICRO
    courier_full, courier_gain_full, heads_full, merge_full, projection_full = (
        lax.all_gather(courier, "fsdp", axis=0, tiled=True),
        lax.all_gather(courier_gain, "fsdp", axis=0, tiled=True),
        lax.all_gather(courier_heads, "fsdp", axis=0, tiled=True),
        lax.all_gather(courier_merge, "fsdp", axis=0, tiled=True),
        lax.all_gather(projection, "fsdp", axis=0, tiled=True),
    )

    def fetch():
        return (
            lax.all_gather(attend_gain, "fsdp", axis=0, tiled=True),
            lax.all_gather(attend_heads, "fsdp", axis=0, tiled=True),
            lax.all_gather(attend_merge, "fsdp", axis=0, tiled=True),
            lax.all_gather(expand_gain, "fsdp", axis=0, tiled=True),
            lax.all_gather(expand_weight, "fsdp", axis=0, tiled=True),
            lax.all_gather(shrink_weight, "fsdp", axis=0, tiled=True),
        )

    leaders = lax.all_gather(patches[:, :, 0, :], "dp", axis=1, tiled=True)
    present = lax.broadcasted_iota(jnp.int32, (videos, frame_total), 1) < counts[:, None]
    message = jnp.einsum("vfd,de->vfe", leaders, courier_full, preferred_element_type=jnp.float32)
    message_norm = layer_norm(message, courier_gain_full).astype(jnp.bfloat16)
    message_mixed = jnp.einsum(
        "vfd,de->vfe", message_norm, heads_full, preferred_element_type=jnp.float32
    )
    told_queries, told_keys, told_values = split_heads(message_mixed, frame_total)
    told, told_normalizer, told_shares = attend_forward(
        told_queries, told_keys, told_values, present
    )
    message_out = message + jnp.einsum(
        "vfd,de->vfe", told, merge_full, preferred_element_type=jnp.float32
    )
    mine = lax.dynamic_slice_in_dim(message_out, offset, local_frames, 1).reshape(rows, width)
    flat = patches.reshape(rows, patch_count, width)
    frame_weights = fetch()
    kept_blocks = []
    sums = []
    for index in range(MICRO):
        if index > 0:
            frame_weights = fetch()
        start = index * per_block
        frame_sums, kept = frame_forward(
            flat[start : start + per_block], mine[start : start + per_block], frame_weights
        )
        kept_blocks.append(kept)
        sums.append(frame_sums)
    frame_sums = jnp.concatenate(sums, 0).reshape(videos, local_frames, width)
    own_present = lax.dynamic_slice_in_dim(present, offset, local_frames, 1)
    partial_value = jnp.sum(jnp.where(own_present[:, :, None], frame_sums, 0.0), 1)
    pooled_sum = lax.psum(partial_value, "dp")
    denominator = (counts * patch_count).astype(jnp.float32)[:, None]
    pooled = pooled_sum / denominator
    pooled_low = pooled.astype(jnp.bfloat16)
    embed = jnp.dot(pooled_low, projection_full, preferred_element_type=jnp.float32)
    video_unit = unit_rows(embed).astype(jnp.bfloat16)
    segment = lax.axis_index("dp") * (captions.shape[0] * lax.axis_size("fsdp"))

    def scores_for(piece):
        text_unit = unit_rows(piece.astype(jnp.float32)).astype(jnp.bfloat16)
        logits = (
            jnp.einsum("ve,te->vt", video_unit, text_unit, preferred_element_type=jnp.float32)
            * LOGIT_SCALE
        )
        positions = segment + lax.broadcasted_iota(jnp.int32, logits.shape, 1)
        return (text_unit, logits, positions == matches[:, None])

    peak = jnp.full((videos,), -1e30, jnp.float32)
    _, logits, matched = scores_for(lax.all_gather(captions, "fsdp", axis=0, tiled=True))
    fresh = jnp.maximum(peak, jnp.max(logits, 1))
    total = jnp.sum(jnp.exp(logits - fresh[:, None]), 1)
    picked = jnp.sum(jnp.where(matched, logits, 0.0), 1)
    peak, total, picked = (fresh, total, picked)

    def combine(first, second):
        top = jnp.maximum(first[0], second[0])
        joined = first[1] * jnp.exp(first[0] - top) + second[1] * jnp.exp(second[0] - top)
        return (top, joined, first[2] + second[2])

    peak, total, picked = joined_2((peak, total, picked), "dp", combine)
    normalizer = peak + jnp.log(total)
    loss = normalizer - picked
    text_unit, logits, matched = scores_for(lax.all_gather(captions, "fsdp", axis=0, tiled=True))
    slope = (jnp.exp(logits - normalizer[:, None]) - matched.astype(jnp.float32)).astype(
        jnp.bfloat16
    )
    unit_grad = jnp.dot(slope, text_unit, preferred_element_type=jnp.float32) * LOGIT_SCALE
    unit_grad = lax.psum(unit_grad, "dp")
    _, unit_pull = jax.vjp(unit_rows, embed)
    embed_grad = unit_pull(unit_grad)[0].astype(jnp.bfloat16)
    projection_grad = jnp.einsum(
        "vd,ve->de", pooled_low, embed_grad, preferred_element_type=jnp.float32
    )
    pooled_grad = jnp.einsum(
        "ve,de->vd", embed_grad, projection_full, preferred_element_type=jnp.float32
    )
    upstream_all = jnp.where(own_present[:, :, None], (pooled_grad / denominator)[:, None, :], 0.0)
    upstream_all = upstream_all.reshape(rows, width)
    collected = None
    patch_list = []
    message_list = []
    for index in range(MICRO):
        frame_weights = fetch()
        start = index * per_block
        patch_grad, message_token_grad, block_grads = frame_backward(
            kept_blocks[index], upstream_all[start : start + per_block], frame_weights
        )
        patch_list.append(patch_grad)
        message_list.append(message_token_grad)
        block_grads = (
            lax.psum_scatter(
                block_grads[0].astype(jnp.float32), "fsdp", scatter_dimension=0, tiled=True
            ),
            lax.psum_scatter(block_grads[1], "fsdp", scatter_dimension=0, tiled=True),
            lax.psum_scatter(block_grads[2], "fsdp", scatter_dimension=0, tiled=True),
            lax.psum_scatter(
                block_grads[3].astype(jnp.float32), "fsdp", scatter_dimension=0, tiled=True
            ),
            lax.psum_scatter(block_grads[4], "fsdp", scatter_dimension=0, tiled=True),
            lax.psum_scatter(block_grads[5], "fsdp", scatter_dimension=0, tiled=True),
        )
        collected = (
            block_grads if collected is None else jax.tree.map(jnp.add, collected, block_grads)
        )
    collected = (
        lax.psum(collected[0].astype(jnp.bfloat16), "dp").astype(jnp.float32),
        lax.psum(collected[1].astype(jnp.bfloat16), "dp").astype(jnp.float32),
        lax.psum(collected[2].astype(jnp.bfloat16), "dp").astype(jnp.float32),
        lax.psum(collected[3].astype(jnp.bfloat16), "dp").astype(jnp.float32),
        lax.psum(collected[4].astype(jnp.bfloat16), "dp").astype(jnp.float32),
        lax.psum(collected[5].astype(jnp.bfloat16), "dp").astype(jnp.float32),
    )
    message_token_grad = jnp.concatenate(message_list, 0).reshape(videos, local_frames, width)
    out_grad = lax.all_gather(message_token_grad, "dp", axis=1, tiled=True)
    out_low = out_grad.astype(jnp.bfloat16)
    merge_message_grad = jnp.einsum(
        "vfd,vfe->de", told, out_low, preferred_element_type=jnp.float32
    )
    told_grad = jnp.einsum("vfe,de->vfd", out_low, merge_full, preferred_element_type=jnp.float32)
    told_query_grad, told_key_grad, told_value_grad = attend_backward(
        told_queries, told_keys, told_values, present, told_normalizer, told_shares, told_grad
    )
    courier_mixed_grad = jnp.concatenate(
        [told_query_grad, told_key_grad, told_value_grad], 2
    ).astype(jnp.bfloat16)
    heads_message_grad = jnp.einsum(
        "vfd,vfe->de", message_norm, courier_mixed_grad, preferred_element_type=jnp.float32
    )
    message_norm_grad = jnp.einsum(
        "vfe,de->vfd", courier_mixed_grad, heads_full, preferred_element_type=jnp.float32
    )
    message_grad, courier_gain_grad = norm_back(message, courier_gain_full, message_norm_grad)
    message_grad = (message_grad + out_grad).astype(jnp.bfloat16)
    courier_grad = jnp.einsum(
        "vfd,vfe->de", leaders, message_grad, preferred_element_type=jnp.float32
    )
    leader_grad = jnp.einsum(
        "vfe,de->vfd", message_grad, courier_full, preferred_element_type=jnp.float32
    )
    own_leader = lax.dynamic_slice_in_dim(leader_grad, offset, local_frames, 1).reshape(rows, width)
    patch_all = jnp.concatenate(patch_list, 0)
    patch_all = patch_all.at[:, 0, :].add(own_leader)
    patch_out = patch_all.reshape(videos, local_frames, patch_count, width).astype(jnp.bfloat16)
    video_grads = (
        lax.psum_scatter(courier_grad, "fsdp", scatter_dimension=0, tiled=True),
        lax.psum_scatter(
            courier_gain_grad.astype(jnp.float32), "fsdp", scatter_dimension=0, tiled=True
        ),
        lax.psum_scatter(heads_message_grad, "fsdp", scatter_dimension=0, tiled=True),
        lax.psum_scatter(merge_message_grad, "fsdp", scatter_dimension=0, tiled=True),
        lax.psum_scatter(projection_grad, "fsdp", scatter_dimension=0, tiled=True),
    )
    return (
        loss,
        patch_out,
        video_grads[0],
        video_grads[1],
        video_grads[2],
        video_grads[3],
        collected[0],
        collected[1],
        collected[2],
        collected[3],
        collected[4],
        collected[5],
        video_grads[4],
    )


def solution(mesh):
    return jax.shard_map(
        shards,
        mesh=mesh,
        in_specs=(
            P("fsdp", "dp", None, None),
            P("fsdp"),
            P(("dp", "fsdp"), None),
            P("fsdp"),
            P("fsdp", None),
            P("fsdp"),
            P("fsdp", None),
            P("fsdp", None),
            P("fsdp"),
            P("fsdp", None),
            P("fsdp", None),
            P("fsdp"),
            P("fsdp", None),
            P("fsdp", None),
            P("fsdp", None),
        ),
        out_specs=(
            P("fsdp"),
            P("fsdp", "dp", None, None),
            P("fsdp", None),
            P("fsdp"),
            P("fsdp", None),
            P("fsdp", None),
            P("fsdp"),
            P("fsdp", None),
            P("fsdp", None),
            P("fsdp"),
            P("fsdp", None),
            P("fsdp", None),
            P("fsdp", None),
        ),
        check_vma=False,
    )
```

profile of v0, /device:TPU:0, one launch (start us, length us, event | category | flops | bytes accessed | tf_op | source)
XLA Modules:
  0.0 1504.3 jit_solution(9632843622007390035)
XLA Ops:
  12.0 2.6 bitcast_convert_fusion.1
  18.7 23.5 %all-reduce.13 = (bf16[768]{0:T(1024)(128)(2,1)S(1)}, bf16[768]{0:T(1024)(128)(2,1)S(1)}, bf16[768]{0:T(1024)(128)(2,1)S(1)}) all-reduce(bf16[768]{0:T(1024)(128)(2,1)S(1)} %dynamic-update-slice.4, bf16[768]{0:T(1024)(128)(2,1)S(1)} %dynamic-update-slice.5, ...), channel_id=1, replica_groups=mesh['dp'=4,'fsdp'=8] {'fsdp'}, use_global_device_ids=true, to_apply=%add.2 | all-reduce | flops 2304 | bytes 9216
  42.2 26.2 %all-gather.2 = bf16[8,1,512]{2,1,0:T(2,128)(2,1)S(1)} all-gather(bf16[1,1,512]{2,1,0:T(2,128)(2,1)S(1)} %bitcast.315), channel_id=1, replica_groups=mesh['dp'=4,'fsdp'=8] {'fsdp'}, dimensions={0}, use_global_device_ids=true | all-gather | bytes 9216 | tf_op jit(solution)/shard_map/all_gather | solution.py:287
  69.3 5.2 all-gather
  74.5 34.5 %all_gather.90 = bf16[768,512]{1,0:T(8,128)(2,1)S(1)} all-gather(bf16[96,512]{1,0:T(8,128)(2,1)S(1)} %copy-done.95), channel_id=1, replica_groups=mesh['dp'=4,'fsdp'=8] {'fsdp'}, dimensions={0}, use_global_device_ids=true | all-gather | bytes 884736 | tf_op jit(solution)/shard_map/all_gather | solution.py:225
  111.4 16.7 %all-gather.14.cloned.1.call-done = bf16[768,2304]{1,0:T(8,128)(2,1)} async-done(((bf16[96,2304]{1,0:T(8,128)(2,1)}), bf16[768,2304]{1,0:T(8,128)(2,1)}) %all-gather.14.cloned.1.call-update) | async-done | bytes 3538960 | tf_op jit(solution)/shard_map/all_gather | solution.py:223
  128.2 2.6 fusion.30
  132.4 39.5 %all-gather.16.cloned.1.call-done = bf16[768,768]{1,0:T(8,128)(2,1)} async-done(((bf16[96,768]{1,0:T(8,128)(2,1)}), bf16[768,768]{1,0:T(8,128)(2,1)}) %all-gather.16.cloned.1.call-update) | async-done | bytes 1179664 | tf_op jit(solution)/shard_map/all_gather | solution.py:224
  174.7 4.2 multiply_reduce_fusion.9
  182.2 4.6 multiply_convert_fusion.9
  186.8 51.1 %all-gather.18.cloned.1.call-done = bf16[768,2304]{1,0:T(8,128)(2,1)} async-done(((bf16[96,2304]{1,0:T(8,128)(2,1)}), bf16[768,2304]{1,0:T(8,128)(2,1)}) %all-gather.18.cloned.1.call-update) | async-done | bytes 3538960 | tf_op jit(solution)/shard_map/all_gather | solution.py:231
  237.9 3.8 convolution_convert_fusion.1
  250.4 3.6 convolution_convert_fusion
  258.3 2.5 copy.554
  260.9 2.5 multiply_reduce_fusion.2
  269.8 9.7 all-gather.20.cloned.1.call-done
  284.2 2.7 multiply_reduce_fusion.3
  300.9 5.4 multiply_convert_fusion.11
  306.3 54.0 %all-gather.22.cloned.1.call-done = bf16[768,3072]{1,0:T(8,128)(2,1)} async-done(((bf16[96,3072]{1,0:T(8,128)(2,1)}), bf16[768,3072]{1,0:T(8,128)(2,1)}) %all-gather.22.cloned.1.call-update) | async-done | bytes 4718608 | tf_op jit(solution)/shard_map/all_gather | solution.py:234
  360.2 8.9 convert_reduce_fusion
  369.2 71.3 %all-gather.24.cloned.1.call-done = bf16[3072,768]{1,0:T(8,128)(2,1)} async-done(((bf16[384,768]{1,0:T(8,128)(2,1)}), bf16[3072,768]{1,0:T(8,128)(2,1)}) %all-gather.24.cloned.1.call-update) | async-done | bytes 4718608 | tf_op jit(solution)/shard_map/all_gather | solution.py:235
  440.5 5.3 fusion.8
  446.6 5.0 convert_reduce_fusion.1
  454.0 5.7 psum.56
  466.1 2.5 dynamic-update-slice.9
  469.1 2.4 dynamic-update-slice.8
  471.5 7.3 all-reduce.12
  482.0 25.6 %while.15 = (s32[]{:T(128)}, f32[1]{0:T(128)}, f32[1]{0:T(128)}, f32[1]{0:T(128)}, f32[3,1]{0,1:T(1,128)}, /*index=5*/f32[3,1]{0,1:T(1,128)S(1)}, f32[3,1]{0,1:T(1,128)}, s32[]{:T(128)}) while((s32[]{:T(128)}, f32[1]{0:T(128)}, f32[1]{0:T(128)}, f32[1]{0:T(128)}, f32[3,1]{0,1:T(1,128)}, /*index=5*/f32[3,1]{0,1:T(1,128)S(1)}, ...), condition=%wide.region_26.27_spmd, body=%wide.region_25.26_spmd.sunk | while | flops 9 | bytes 233 | solution.py:19
  509.7 6.1 psum.57
  519.5 3.7 fusion.117
  523.2 3.8 fusion.113
  527.1 6.0 fusion.12
  533.2 3.6 fusion.14
  536.8 5.4 multiply_reduce_fusion.12
  544.6 5.5 fusion.155
  554.6 3.5 convolution_convert_fusion.4
  564.1 4.1 bitcast_add_fusion.2
  568.3 3.2 convolution_convert_fusion.3
  571.6 2.3 copy.589
  573.9 4.3 multiply_reduce_fusion
  584.0 3.3 multiply_convert_fusion.4
  589.6 4.3 multiply_reduce_fusion.1
  598.2 2.4 multiply_convert_fusion.6
  600.9 3.6 fusion.66
  604.5 5.2 bitcast_add_fusion.1
  610.8 5.3 fusion.61
  616.1 9.5 bitcast_add_fusion
  627.1 5.1 convolution_add_fusion
  633.5 3.8 fusion.24
  639.3 5.9 multiply_reduce_fusion.6
  647.4 120.0 %reduce-scatter.17.cloned.1.call-done = f32[96,2304]{1,0:T(8,128)} async-done(((f32[768,2304]{1,0:T(8,128)}), f32[96,2304]{1,0:T(8,128)}) %reduce-scatter.17.cloned.1.call-update) | async-done | bytes 884752 | tf_op jit(solution)/shard_map/reduce_scatter | solution.py:332
  769.3 164.4 %reduce-scatter.21.cloned.1.call-done = f32[96,3072]{1,0:T(8,128)} async-done(((f32[768,3072]{1,0:T(8,128)}), f32[96,3072]{1,0:T(8,128)}) %reduce-scatter.21.cloned.1.call-update) | async-done | bytes 1179664 | tf_op jit(solution)/shard_map/reduce_scatter | solution.py:337
  935.9 164.5 %reduce-scatter.23.cloned.1.call-done = f32[384,768]{1,0:T(8,128)} async-done(((f32[3072,768]{1,0:T(8,128)}), f32[384,768]{1,0:T(8,128)}) %reduce-scatter.23.cloned.1.call-update) | async-done | bytes 1179664 | tf_op jit(solution)/shard_map/reduce_scatter | solution.py:338
  1102.6 9.4 fusion.151
  1116.2 5.6 all-gather.3
  1123.7 3.2 multiply_reduce_fusion.17
  1129.1 3.1 copy.624
  1135.0 4.0 fusion.143
  1144.7 35.5 %all-reduce.11 = (f32[768]{0:T(1024)S(1)}, bf16[768]{0:T(1024)(128)(2,1)S(1)}, bf16[768]{0:T(1024)(128)(2,1)S(1)}) all-reduce(bf16[768]{0:T(1024)(128)(2,1)S(1)} %get-tuple-element.179, f32[768]{0:T(1024)S(1)} %convert_add_fusion.1, f32[768]{0:T(1024)S(1)} %convert_add_fusion), channel_id=11, replica_groups=mesh['dp'=4,'fsdp'=8] {'fsdp'}, use_global_device_ids=true, to_apply=%region_44.45.clone | all-reduce | flops 2304 | bytes 13824
  1180.9 6.0 all-reduce.14
  1193.9 25.3 %reduce-scatter.15.cloned.1.call-done = f32[96,512]{1,0:T(8,128)} async-done(((f32[768,512]{1,0:T(8,128)}), f32[96,512]{1,0:T(8,128)}) %reduce-scatter.15.cloned.1.call-update) | async-done | bytes 196624 | tf_op jit(solution)/shard_map/reduce_scatter | solution.py:389
  1219.2 72.2 %reduce-scatter.25.cloned.1.call-done = f32[96,768]{1,0:T(8,128)} async-done(((f32[768,768]{1,0:T(8,128)}), f32[96,768]{1,0:T(8,128)}) %reduce-scatter.25.cloned.1.call-update) | async-done | bytes 294928
  1291.4 72.4 %reduce-scatter.13.cloned.1.call-done = f32[96,768]{1,0:T(8,128)} async-done(((f32[768,768]{1,0:T(8,128)}), f32[96,768]{1,0:T(8,128)}) %reduce-scatter.13.cloned.1.call-update) | async-done | bytes 294928 | tf_op jit(solution)/shard_map/reduce_scatter | solution.py:388
  1363.8 132.6 %reduce-scatter.11.cloned.1.call-done = f32[96,2304]{1,0:T(8,128)} async-done(((f32[768,2304]{1,0:T(8,128)}), f32[96,2304]{1,0:T(8,128)}) %reduce-scatter.11.cloned.1.call-update) | async-done | bytes 884752 | tf_op jit(solution)/shard_map/reduce_scatter | solution.py:387
  (543 shorter events, 140.2 us)
Async XLA Ops:
  7.2 102.4 %all-gather.12.cloned.1.call-start = ((), (), s32[]{:S(2)}) async-start(), calls=%async_computation.8 | async-start | bytes 1327104 | tf_op jit(solution)/shard_map/all_gather | solution.py:221
  7.9 120.2 %all-gather.14.cloned.1.call-start = ((), (), s32[]{:S(2)}) async-start(), calls=%async_computation.9 | async-start | bytes 3981312 | tf_op jit(solution)/shard_map/all_gather | solution.py:223
  8.7 163.2 %all-gather.16.cloned.1.call-start = ((), (), s32[]{:S(2)}) async-start(), calls=%async_computation.10 | async-start | bytes 1327104 | tf_op jit(solution)/shard_map/all_gather | solution.py:224
  9.4 228.5 %all-gather.18.cloned.1.call-start = ((), (), s32[]{:S(2)}) async-start(), calls=%async_computation.11 | async-start | bytes 3981312 | tf_op jit(solution)/shard_map/all_gather | solution.py:231
  10.0 269.5 %all-gather.20.cloned.1.call-start = ((), (), s32[]{:S(2)}) async-start(), calls=%async_computation.12 | async-start | bytes 1327104 | tf_op jit(solution)/shard_map/all_gather | solution.py:232
  10.6 349.7 %all-gather.22.cloned.1.call-start = ((), (), s32[]{:S(2)}) async-start(), calls=%async_computation.13 | async-start | bytes 5308416 | tf_op jit(solution)/shard_map/all_gather | solution.py:234
  11.1 429.3 %all-gather.24.cloned.1.call-start = ((), (), s32[]{:S(2)}) async-start(), calls=%async_computation.14 | async-start | bytes 5308416 | tf_op jit(solution)/shard_map/all_gather | solution.py:235
  11.9 633.8 %reduce-scatter.19.cloned.1.call-start = ((), (), s32[]{:S(2)}) async-start(), calls=%async_computation.19 | async-start | bytes 2654208 | tf_op jit(solution)/shard_map/reduce_scatter | solution.py:333
  12.0 6.2 copy-start.135
  12.0 6.5 copy-start.136
  12.0 30.2 %slice-start.7 = ((bf16[1,4,197,768]{3,1,2,0:T(4,128)(2,1)}), bf16[1,4,1,768]{3,1,2,0:T(4,128)(2,1)S(1)}, s32[]{:S(2)}) async-start(bf16[1,4,197,768]{3,1,2,0:T(4,128)(2,1)} %param.19), calls=%async_computation.31 | async-start | bytes 12288 | tf_op jit(solution)/shard_map/slice | solution.py:238
  12.0 30.2 %copy-start.126 = (bf16[1,512]{1,0:T(2,128)(2,1)S(1)}, bf16[1,512]{1,0:T(2,128)(2,1)}, u32[]{:S(2)}) copy-start(bf16[1,512]{1,0:T(2,128)(2,1)} %param.21) | copy-start | bytes 3076
  12.0 62.5 %copy-start.95 = (bf16[96,512]{1,0:T(8,128)(2,1)S(1)}, bf16[96,512]{1,0:T(8,128)(2,1)}, u32[]{:S(2)}) copy-start(bf16[96,512]{1,0:T(8,128)(2,1)} %param.33) | copy-start | bytes 294916
  14.7 167.5 %copy-start.2 = (f32[2,197,768]{2,0,1:T(2,128)}, f32[2,197,768]{2,0,1:T(2,128)S(1)}, u32[]{:S(2)}) copy-start(f32[2,197,768]{2,0,1:T(2,128)S(1)} %get-tuple-element.241) | copy-start | bytes 3631108
  42.2 88.6 %copy-start.79 = (f32[768]{0:T(1024)}, f32[768]{0:T(1024)S(1)}, u32[]{:S(2)}) copy-start(f32[768]{0:T(1024)S(1)} %convert_element_type.269) | copy-start | bytes 9220
  42.2 140.0 %copy-start.96 = (f32[768]{0:T(1024)}, f32[768]{0:T(1024)S(1)}, u32[]{:S(2)}) copy-start(f32[768]{0:T(1024)S(1)} %convert_element_type.278) | copy-start | bytes 9220
  74.5 56.3 %copy-start.93 = (bf16[1,16,1,768]{3,2,0,1:T(2,128)(2,1)}, bf16[1,16,1,768]{3,2,0,1:T(2,128)(2,1)S(1)}, u32[]{:S(2)}) copy-start(bf16[1,16,1,768]{3,2,0,1:T(2,128)(2,1)S(1)} %all-gather) | copy-start | bytes 73732
  111.2 62.2 %copy-start.62 = (f32[16,768]{1,0:T(8,128)}, f32[16,768]{1,0:T(8,128)S(1)}, u32[]{:S(2)}) copy-start(f32[16,768]{1,0:T(8,128)S(1)} %get-tuple-element.263) | copy-start | bytes 147460
  111.2 19.6 %copy-start.110 = (f32[16]{0:T(128)}, f32[16]{0:T(128)S(1)}, u32[]{:S(2)}) copy-start(f32[16]{0:T(128)S(1)} %broadcast_multiply_fusion.8) | copy-start | bytes 196
  111.4 19.4 %copy-start.130 = (f32[16]{0:T(128)}, f32[16]{0:T(128)S(1)}, u32[]{:S(2)}) copy-start(f32[16]{0:T(128)S(1)} %multiply_reduce_fusion.19) | copy-start | bytes 196
  111.4 19.4 %copy-start.120 = (f32[16]{0:T(128)}, f32[16]{0:T(128)S(1)}, u32[]{:S(2)}) copy-start(f32[16]{0:T(128)S(1)} %fusion.134) | copy-start | bytes 196
  131.1 43.0 %copy-start.91 = (bf16[16,12,64]{2,1,0:T(8,128)(2,1)}, bf16[16,12,64]{2,1,0:T(8,128)(2,1)S(1)}, u32[]{:S(2)}) copy-start(bf16[16,12,64]{2,1,0:T(8,128)(2,1)S(1)} %reshape.721) | copy-start | bytes 73732
  131.4 40.5 %copy-start.98 = (f32[12,16]{1,0:T(8,128)}, f32[12,16]{1,0:T(8,128)S(1)}, u32[]{:S(2)}) copy-start(f32[12,16]{1,0:T(8,128)S(1)} %get-tuple-element.264) | copy-start | bytes 2308
  132.0 42.6 %copy-start.100 = (f32[12,16]{1,0:T(8,128)}, f32[12,16]{1,0:T(8,128)S(1)}, u32[]{:S(2)}) copy-start(f32[12,16]{1,0:T(8,128)S(1)} %fusion.78) | copy-start | bytes 2308
  132.4 41.7 %copy-start.81 = (bf16[16,768]{1,0:T(8,128)(2,1)}, bf16[16,768]{1,0:T(8,128)(2,1)S(1)}, u32[]{:S(2)}) copy-start(bf16[16,768]{1,0:T(8,128)(2,1)S(1)} %convert_element_type.277) | copy-start | bytes 73732
  173.5 8.7 copy-start.83
  173.5 8.7 copy-start.85
  174.1 8.1 copy-start.45
  174.7 12.1 copy-start.47
  179.9 7.0 copy-start.116
  180.0 6.9 copy-start.114
  243.7 6.8 copy-start.51
  269.8 9.7 copy-start.19
  451.7 9.5 copy-start.102
  461.9 18.2 %copy-start.129 = (f32[8]{0:T(128)}, f32[8]{0:T(128)S(1)}, u32[]{:S(2)}) copy-start(f32[8]{0:T(128)S(1)} %get-tuple-element.275) | copy-start | bytes 100
  517.7 9.4 slice-start.10
  519.5 34.1 %copy-start.108 = (f32[2,768]{1,0:T(2,128)}, f32[2,768]{1,0:T(2,128)S(1)}, u32[]{:S(2)}) copy-start(f32[2,768]{1,0:T(2,128)S(1)} %get-tuple-element.245) | copy-start | bytes 18436
  519.5 7.6 slice-start.11
  523.2 9.9 copy-start.105
  523.2 9.9 slice-start.8
  523.2 9.9 slice-start.12
  568.3 199.1 %reduce-scatter.17.cloned.1.call-start = ((), (), s32[]{:S(2)}) async-start(), calls=%async_computation.18 | async-start | bytes 7962624 | tf_op jit(solution)/shard_map/reduce_scatter | solution.py:332
  571.6 6.6 slice-start
  587.3 6.7 slice-start.2
  609.7 6.3 copy-start.69
  609.8 6.3 copy-start.104
  609.8 324.0 %reduce-scatter.21.cloned.1.call-start = ((), (), s32[]{:S(2)}) async-start(), calls=%async_computation.20 | async-start | bytes 10616832 | tf_op jit(solution)/shard_map/reduce_scatter | solution.py:337
  625.6 474.8 %reduce-scatter.23.cloned.1.call-start = ((), (), s32[]{:S(2)}) async-start(), calls=%async_computation.21 | async-start | bytes 10616832 | tf_op jit(solution)/shard_map/reduce_scatter | solution.py:338
  632.2 555.7 %all-reduce.18.cloned.1.call-start = ((), (), s32[]{:S(2)}) async-start(), calls=%async_computation.23 | async-start | bytes 3538944 | tf_op jit(solution)/shard_map/psum | solution.py:345
  639.2 6.3 copy-start.115
  1102.6 9.4 copy-start.125
  1102.6 116.6 %reduce-scatter.15.cloned.1.call-start = ((), (), s32[]{:S(2)}) async-start(), calls=%async_computation.17 | async-start | bytes 1769472 | tf_op jit(solution)/shard_map/reduce_scatter | solution.py:389
  1113.5 177.9 %reduce-scatter.25.cloned.1.call-start = ((), (), s32[]{:S(2)}) async-start(), calls=%async_computation.22 | async-start | bytes 2654208
  1114.1 7.7 copy-start.38
  1114.1 8.3 copy-start.68
  1114.1 8.3 copy-start.88
  1114.1 8.5 copy-start.92
  1116.0 6.9 copy-start.90
  1116.1 7.5 copy-start.63
  1116.1 7.5 copy-start.80
  1116.1 7.5 copy-start.111
  1116.1 7.5 copy-start.121
  1132.3 231.5 %reduce-scatter.13.cloned.1.call-start = ((), (), s32[]{:S(2)}) async-start(), calls=%async_computation.16 | async-start | bytes 2654208 | tf_op jit(solution)/shard_map/reduce_scatter | solution.py:388
  1134.9 361.5 %reduce-scatter.11.cloned.1.call-start = ((), (), s32[]{:S(2)}) async-start(), calls=%async_computation.15 | async-start | bytes 7962624 | tf_op jit(solution)/shard_map/reduce_scatter | solution.py:387
  (104 other events, 308.2 us)
Sparse Core Ops, SparseCore 0:
  10.2 43.8 all-gather.11
  56.3 71.8 all-gather.13
  130.3 41.4 all-gather.15
  173.9 63.9 all-gather.17
  239.9 39.5 all-gather.19
  281.6 78.6 all-gather.21
  362.4 78.0 all-gather.23
  568.4 67.1 reduce-scatter.18
  639.3 128.0 reduce-scatter.16
  771.2 162.4 reduce-scatter.20
  937.8 162.5 reduce-scatter.22
  1104.2 45.9 all-reduce.17
  1154.2 64.9 reduce-scatter.14
  1223.5 67.8 reduce-scatter.24
  1295.7 68.0 reduce-scatter.12
  1368.3 128.0 reduce-scatter.10
where the time goes:
time: 1510 us; the launch traced here: 1500 us
  waiting for transfers between devices  998 us (66%)
  blocking collectives  155 us (10%)
  matrix products  143 us (9%)
  other arithmetic  90.5 us (6%)
  local copies, waits for them, and re-layouts  73.2 us (5%)
  between operations  24.5 us (2%)
  loops' own time  18.3 us (1%)
    reduce_scatter x1, waiting for transfers between devices, shards(): lax.psum_scatter(block_grads[5], 'fsdp', scatter_dimension=0, tiled=True)  164 us
    reduce_scatter x1, waiting for transfers between devices, shards(): lax.psum_scatter(block_grads[4], 'fsdp', scatter_dimension=0, tiled=True)  164 us
    reduce_scatter x1, waiting for transfers between devices, shards(): lax.psum_scatter(heads_message_grad, 'fsdp', scatter_dimension=0, tiled=T...  133 us
    reduce_scatter x1, waiting for transfers between devices, shards(): lax.psum_scatter(block_grads[1], 'fsdp', scatter_dimension=0, tiled=True)  120 us
    unnamed x17, waiting for transfers between devices  76.7 us
    reduce_scatter x1, waiting for transfers between devices, shards(): lax.psum_scatter(merge_message_grad, 'fsdp', scatter_dimension=0, tiled=T...  72.4 us
    all_gather x1, waiting for transfers between devices, fetch(): lax.all_gather(shrink_weight, 'fsdp', axis=0, tiled=True)  71.3 us
    unnamed x3, blocking collectives  66.2 us
  transfers between devices with their start and end apart: 16, of which 13 were waited for; matrix products, arithmetic and copies ran while one was open for 14% of the time, Pallas kernels for 0%

commit v1 on v0

--- a/solution.py
+++ b/solution.py
@@ -1,15 +1,905 @@
+import functools
+
 import jax
 import jax.numpy as jnp
 from jax import lax
+from jax.experimental import pallas as pl
+from jax.experimental.pallas import tpu as pltpu
 from jax.sharding import PartitionSpec as P
 
+MESH = pl.DeviceIdType.MESH
+Z, Y = 4, 2
 HEADS = 12
 HEAD = 64
-MICRO = 2
-
-
 EPSILON = 1e-05
 LOGIT_SCALE = 64.0
+PAD = 208
+ROWS = 832
+D = 768
+F32 = jnp.float32
+B16 = jnp.bfloat16
+
+MICRO = 2
+
+COURIER, GAINS, CHEADS, AHEADS, CMERGE, AMERGE, EXPAND, PROJ = 0, 768, 896, 3200, 5504, 6272, 7040, 10112
+NCOLS = 10624
+JOBS = ((0, 896), (896, 768), (1664, 768), (2432, 768), (3200, 768), (3968, 768), (4736, 768), (5504, 768), (6272, 768),
+        (7040, 768), (7808, 768), (8576, 768), (9344, 768), (10112, 512))
+
+
+class Pos:
+    def __init__(self):
+        self.dp = lax.axis_index("dp")
+        self.k = lax.axis_index("fsdp")
+        self.x, self.c = self.dp // 2, lax.rem(self.dp, 2)
+        self.z, self.y = self.k // Y, lax.rem(self.k, Y)
+        self.core = (self.x * 2 + 1 - self.c, self.k)
+        self.xp = ((1 - self.x) * 2 + self.c, self.k)
+        self.cross = ((1 - self.x) * 2 + 1 - self.c, self.k)
+        self.yp = (self.dp, self.z * Y + 1 - self.y)
+        self.team = (self.core, self.xp, self.cross)
+
+    def ahead(self, d):
+        return lax.rem(self.z + d, Z)
+
+    def behind(self, d):
+        return lax.rem(self.z - d + Z, Z)
+
+    def column(self):
+        return [(self.dp, self.ahead(d) * Y + self.y) for d in (1, 2, 3)]
+
+    def peers(self):
+        return [self.core, self.xp, self.yp] + self.column()
+
+    def plane(self):
+        return [(self.dp, lax.rem(self.k + d, Z * Y)) for d in range(1, Z * Y)]
+
+
+def barrier(peers):
+    semaphore = pltpu.get_barrier_semaphore()
+    for peer in peers:
+        pl.semaphore_signal(semaphore, inc=1, device_id=peer, device_id_type=MESH)
+    pl.semaphore_wait(semaphore, len(peers))
+
+
+def remote(source, target, send, receive, device):
+    return pltpu.make_async_remote_copy(
+        src_ref=source, dst_ref=target, send_sem=send, recv_sem=receive, device_id=device, device_id_type=MESH)
+
+
+class Gather:
+    def __init__(self, p, block, jobs, send, receive):
+        self.p, self.block, self.jobs, self.send, self.receive = p, block, jobs, send, receive
+
+    def copy(self, job, index, k, first, count, device):
+        ref = self.block(k, first, count, job)
+        return remote(ref, ref, self.send.at[job, index], self.receive.at[job, index], device)
+
+    def far(self, d):
+        p = self.p
+        return p.behind(d + 1) * Y + p.y if d < 3 else p.behind(d - 3) * Y + 1 - p.y
+
+    def stage(self, stage, job):
+        if job < 0 or job >= self.jobs:
+            return
+        p, copy = self.p, self.copy
+        own, single = 3 * p.c + p.x, 3 * p.c + 2 * p.x
+        other = 3 * p.c + 2 * (1 - p.x)
+        if stage == 0:
+            for d, device in enumerate(p.column()):
+                copy(job, d, p.k, own, 2, device).start()
+            copy(job, 3, p.k, own, 2, p.yp).start()
+        elif stage == 1:
+            for d in range(3):
+                k = self.far(d)
+                copy(job, d, k, own, 2, p.core).wait_recv()
+                copy(job, 4 + d, k, own, 2, p.yp).start()
+                copy(job, 7 + d, k, single, 1, p.xp).start()
+                copy(job, 14 + d, k, own, 2, p.core).start()
+        elif stage == 2:
+            for d in range(3, 7):
+                k = self.far(d)
+                copy(job, d, k, own, 2, p.core).wait_recv()
+                copy(job, 7 + d, k, single, 1, p.xp).start()
+                copy(job, 14 + d, k, own, 2, p.core).start()
+        elif stage == 3:
+            for d in range(7):
+                k = self.far(d)
+                copy(job, 7 + d, k, other, 1, p.core).wait_recv()
+                copy(job, 21 + d, k, other, 1, p.core).start()
+        elif stage == 4:
+            for d in range(7):
+                copy(job, 14 + d, self.far(d), 3 * (1 - p.c) + p.x, 2, p.core).wait_recv()
+            for d in range(7):
+                copy(job, 21 + d, self.far(d), 3 * (1 - p.c) + 2 * (1 - p.x), 1, p.core).wait_recv()
+        elif stage == 5:
+            for index in range(28):
+                copy(job, index, p.k, 0, 2 if index < 7 or 14 <= index < 21 else 1, p.core).wait_send()
+
+    def tick(self, t, lag):
+        for stage in (5, 4, 3, 2, 1, 0):
+            self.stage(stage, t - lag[stage])
+
+
+class Spread:
+    def __init__(self, p, source, target, send, receive, same=False):
+        self.p, self.target = p, target
+        count = Z * Y
+        self.copies = []
+        for d in range(1, count):
+            to = lax.rem(p.k + d, count)
+            part = source if same else source.at[to]
+            self.copies.append(remote(part, target.at[p.k], send.at[d - 1], receive.at[d - 1], (p.dp, to)))
+        self.arrivals = []
+        for d in range(1, count):
+            origin = lax.rem(p.k - d + count, count)
+            self.arrivals.append(
+                remote(target.at[origin], target.at[origin], send.at[d - 1], receive.at[d - 1], (p.dp, origin)))
+        target[p.k] = source[...] if same else source[p.k]
+        for copy in self.copies:
+            copy.start()
+
+    def wait(self):
+        for copy in self.arrivals:
+            copy.wait_recv()
+
+    def done(self):
+        for copy in self.copies:
+            copy.wait_send()
+
+
+class Team:
+    def __init__(self, p, source, target, send, receive):
+        self.copies, self.arrivals = [], []
+        target[p.dp] = source[...]
+        for index, other in enumerate(p.team):
+            self.copies.append(remote(source, target.at[p.dp], send.at[index], receive.at[index], other))
+            self.arrivals.append(remote(source, target.at[other[0]], send.at[index], receive.at[index], other))
+        for copy in self.copies:
+            copy.start()
+
+    def wait(self):
+        for copy in self.arrivals:
+            copy.wait_recv()
+
+    def done(self):
+        for copy in self.copies:
+            copy.wait_send()
+
+
+class Reduce:
+    def __init__(self, p, stage, buffers, out, jobs, send, receive):
+        self.p, self.stage, self.out, self.jobs, self.send, self.receive = p, stage, out, jobs, send, receive
+        self.rc, self.rx, self.ry, self.rz, self.own, self.rf, self.fin, self.rcf = buffers
+
+    def copies(self, job, step):
+        p = self.p
+        first, count = self.jobs[job]
+        cols = pl.ds(first, count)
+        half, other = pl.ds(pl.multiple_of(48 * p.c, 16), 48), pl.ds(pl.multiple_of(48 * (1 - p.c), 16), 48)
+        carried = pl.ds(pl.multiple_of((3 * p.c + p.x) * 16, 16), 32)
+        away = pl.ds(pl.multiple_of((3 * p.c + 2 * (1 - p.x)) * 16, 16), 16)
+        s, r = self.send, self.receive
+        if step == 0:
+            return [remote(self.stage.at[:, other, cols], self.rc.at[:, :, cols], s.at[job, 0], r.at[job, 0], p.core)]
+        if step == 1:
+            return [remote(self.stage.at[:, away, cols], self.rx.at[:, :, cols], s.at[job, 1], r.at[job, 1], p.xp)]
+        if step == 2:
+            return [remote(self.stage.at[z * Y + 1 - p.y, carried, cols], self.ry.at[z, :, cols], s.at[job, 2 + z],
+                           r.at[job, 2 + z], p.yp) for z in range(Z)]
+        if step == 3:
+            return [remote(self.stage.at[device[1], carried, cols], self.rz.at[d, :, cols], s.at[job, 6 + d],
+                           r.at[job, 6 + d], device) for d, device in enumerate(p.column())]
+        if step == 4:
+            return [remote(self.own.at[:, cols], self.rf.at[:, cols], s.at[job, 9], r.at[job, 9], p.xp)]
+        return [remote(self.fin.at[half, cols], self.rcf.at[:, cols], s.at[job, 10], r.at[job, 10], p.core)]
+
+    def step(self, step, job):
+        if job < 0 or job >= len(self.jobs):
+            return
+        p = self.p
+        first, count = self.jobs[job]
+        cols = pl.ds(first, count)
+        if step > 0 and step < 7:
+            for copy in self.copies(job, step - 1):
+                copy.wait_recv()
+        if step == 1:
+            half = pl.ds(pl.multiple_of(48 * p.c, 16), 48)
+            for k in range(Z * Y):
+                self.stage[k, half, cols] = (self.stage[k, half, cols].astype(F32) + self.rc[k, :, cols].astype(F32)).astype(B16)
+        elif step == 2:
+            single = pl.ds(pl.multiple_of((3 * p.c + 2 * p.x) * 16, 16), 16)
+            for k in range(Z * Y):
+                self.stage[k, single, cols] = (self.stage[k, single, cols].astype(F32) + self.rx[k, :, cols].astype(F32)).astype(B16)
+        elif step == 3:
+            carried = pl.ds(pl.multiple_of((3 * p.c + p.x) * 16, 16), 32)
+            for z in range(Z):
+                k = z * Y + p.y
+                self.stage[k, carried, cols] = (self.stage[k, carried, cols].astype(F32) + self.ry[z, :, cols].astype(F32)).astype(B16)
+        elif step == 4:
+            carried = pl.ds(pl.multiple_of((3 * p.c + p.x) * 16, 16), 32)
+            total = self.stage[p.k, carried, cols].astype(F32)
+            for d in range(3):
+                total = total + self.rz[d, :, cols].astype(F32)
+            self.own[:, cols] = total.astype(B16)
+        elif step == 5:
+            mine, theirs = self.own[:, cols].astype(F32), self.rf[:, cols].astype(F32)
+            left = jnp.where(p.x == 0, mine[0:16], theirs[0:16])
+            right = jnp.where(p.x == 0, theirs[16:32], mine[16:32])
+            middle = jnp.where(p.x == 0, mine[16:32], mine[0:16]) + jnp.where(p.x == 0, theirs[0:16], theirs[16:32])
+            half = pl.ds(pl.multiple_of(48 * p.c, 16), 48)
+            self.fin[half, cols] = jnp.concatenate([left, middle, right], 0).astype(B16)
+        elif step == 6:
+            other = pl.ds(pl.multiple_of(48 * (1 - p.c), 16), 48)
+            half = pl.ds(pl.multiple_of(48 * p.c, 16), 48)
+            self.out[half, cols] = self.fin[half, cols].astype(F32)
+            self.out[other, cols] = self.rcf[:, cols].astype(F32)
+        if step < 6:
+            for copy in self.copies(job, step):
+                copy.start()
+        if step == 7:
+            for earlier in range(6):
+                for copy in self.copies(job, earlier):
+                    copy.wait_send()
+
+    def tick(self, t, lag):
+        for step in (7, 6, 5, 4, 3, 2, 1, 0):
+            self.step(step, t - lag[step])
+
+
+def dot(a, b, ca=1, cb=0):
+    return lax.dot_general(a, b, (((ca,), (cb,)), ((), ())), preferred_element_type=F32)
+
+
+def normalize(value):
+    center = value - jnp.mean(value, -1, keepdims=True)
+    rate = lax.rsqrt(jnp.mean(center * center, -1, keepdims=True) + EPSILON)
+    return center * rate, rate
+
+
+def head_mask():
+    return lax.broadcasted_iota(jnp.int32, (192, D), 0) // 16 == lax.broadcasted_iota(jnp.int32, (192, D), 1) // HEAD
+
+
+def spread_heads(value):
+    return jnp.where(head_mask(), jnp.concatenate([value.astype(F32)] * HEADS, 0), 0.0).astype(B16)
+
+
+def join_heads(value):
+    value = jnp.where(head_mask(), value, 0.0)
+    total = value[0:16]
+    for head in range(1, HEADS):
+        total = total + value[16 * head : 16 * head + 16]
+    return total
+
+
+def row_of(value, index):
+    rows = lax.broadcasted_iota(jnp.int32, value.shape, 0)
+    return jnp.sum(jnp.where(rows == index, value, 0.0), 0, keepdims=True)
+
+
+def forward_kernel(
+    xs, lead, caption, counts, courier, gains, cheads, aheads, cmerge, amerge, expand, projection,
+    full_o, normt_o, mixed_o, shares_o, seen_o, seent_o, hidden_o, n2t_o, d_o, gsum_o, hsum_o, gains_o,
+    leaders_o, message_o, mnorm_o, mmix_o, mshare_o, told_o, mout_o, texts_o,
+    full, leadbuf, norm, normt, mixed, shares, seen, seent, hidden, n2, n2t, dd,
+    texts, ssem, rsem, lsem, lead_s, lead_r, text_s, text_r, osem,
+):
+    p = Pos()
+    weights = ((courier, COURIER), (gains, GAINS), (cheads, CHEADS), (aheads, AHEADS), (cmerge, CMERGE), (amerge, AMERGE),
+               (expand, EXPAND), (projection, PROJ))
+    mine = pl.ds(pl.multiple_of(p.k * 96, 16), 96)
+    loads = []
+    for index, (ref, start) in enumerate(weights):
+        copy = pltpu.make_async_copy(ref, full.at[mine, pl.ds(start, ref.shape[1])], lsem.at[index])
+        copy.start()
+        loads.append(copy)
+    leadbuf[p.dp] = lead[...]
+    barrier(p.plane() + list(p.team))
+    text_hop = Spread(p, caption, texts, text_s, text_r, same=True)
+    others = [p.core, p.xp, ((1 - p.x) * 2 + 1 - p.c, p.k)]
+    sends = []
+    for index, other in enumerate(others):
+        copy = pltpu.make_async_remote_copy(
+            src_ref=lead, dst_ref=leadbuf.at[p.dp], send_sem=lead_s.at[0, index], recv_sem=lead_r.at[0, index],
+            device_id=other, device_id_type=MESH)
+        copy.start()
+        sends.append(copy)
+    for copy in loads:
+        copy.wait()
+    def block(k, start, count, job):
+        first_col, columns = JOBS[job]
+        return full.at[pl.ds(pl.multiple_of(k * 96 + start * 16, 16), count * 16), pl.ds(first_col, columns)]
+
+    gather = Gather(p, block, len(JOBS), ssem, rsem)
+    lag = (0, 2, 4, 6, 8, 9)
+    outs = []
+
+    def out(source, target):
+        copy = pltpu.make_async_copy(source, target, osem.at[len(outs)])
+        copy.start()
+        outs.append(copy)
+
+    def ticks(first, last):
+        for t in range(first, last + 1):
+            gather.tick(t, lag)
+
+    ticks(0, 4)
+    text_hop.wait()
+    text_team = Team(p, texts, texts_o, lead_s.at[1], lead_r.at[1])
+    ticks(5, 8)
+    for index, other in enumerate(others):
+        pltpu.make_async_remote_copy(
+            src_ref=lead, dst_ref=leadbuf.at[other[0]], send_sem=lead_s.at[0, index], recv_sem=lead_r.at[0, index],
+            device_id=other, device_id_type=MESH).wait_recv()
+    leaders = jnp.concatenate([leadbuf[index][0:4] for index in range(4)], 0)
+    leaders_o[...] = leaders.astype(B16)
+    rows = jnp.transpose(full[:, GAINS : GAINS + 128].astype(F32))[0:8]
+    gains_o[...] = rows
+    courier_gain, attend_gain, expand_gain = rows[0:1], rows[1:2], rows[2:3]
+    message = dot(leaders.astype(B16), full[:, COURIER : COURIER + D])
+    message_o[...] = message
+    xh, _ = normalize(message)
+    mnorm = (xh * courier_gain).astype(B16)
+    mnorm_o[...] = mnorm
+
+    def norm_frame(f, carry):
+        here = pl.ds(pl.multiple_of(f * PAD, 16), PAD)
+        xh, _ = normalize(xs[f].astype(F32))
+        norm[here, :] = (xh * attend_gain).astype(B16)
+        return carry
+
+    lax.fori_loop(0, 4, norm_frame, 0)
+    ticks(9, 11)
+    mmix = dot(mnorm, full[:, CHEADS : CHEADS + 3 * D])
+    mq, mk, mv = mmix[:, :D].astype(B16), mmix[:, D : 2 * D].astype(B16), mmix[:, 2 * D :].astype(B16)
+    mmix_o[...] = mmix.astype(B16)
+    scores = dot(spread_heads(mq), mk, 1, 1) * HEAD ** (-0.5)
+    frames = lax.broadcasted_iota(jnp.int32, (192, 16), 1)
+    scores = jnp.where(frames < counts[0], scores, -1000000000.0)
+    raised = jnp.exp(scores - jnp.max(scores, -1, keepdims=True))
+    mshare = raised / jnp.sum(raised, -1, keepdims=True)
+    mshare_o[...] = mshare
+    told = join_heads(dot(mshare.astype(B16), mv)).astype(B16)
+    told_o[...] = told
+
+    def heads_tile(base, factor):
+        def body(n, carry):
+            cols = pl.ds(pl.multiple_of(base + n * 256, 256), 256)
+            wcols = pl.ds(pl.multiple_of(AHEADS + base + n * 256, 128), 256)
+            mixed[:, cols] = (dot(norm[...], full[:, wcols]) * factor).astype(B16)
+            return carry
+        lax.fori_loop(0, 3, body, 0)
+
+    ticks(12, 12)
+    heads_tile(0, HEAD ** (-0.5))
+    ticks(13, 13)
+    heads_tile(D, 1.0)
+    ticks(14, 14)
+    heads_tile(2 * D, 1.0)
+    ticks(15, 15)
+    mout_all = message + dot(told, full[:, CMERGE : CMERGE + D])
+    mout = jnp.concatenate([row_of(mout_all, p.dp * 4 + f) for f in range(4)] + [jnp.zeros((4, D), F32)], 0)
+    mout_o[...] = mout
+    xh, _ = normalize(mout)
+    extra = (xh * attend_gain).astype(B16)
+    extra_kv = dot(extra, full[:, AHEADS + D : AHEADS + 3 * D])
+    extra = extra.astype(F32)
+    spot = lax.broadcasted_iota(jnp.int32, (16, 1), 0) == 5
+    for f in range(4):
+        tail = pl.ds(f * PAD + 192, 16)
+        norm[tail, :] = jnp.where(spot, extra[f : f + 1], norm[tail, :].astype(F32)).astype(B16)
+        old = mixed[tail, D : 3 * D].astype(F32)
+        mixed[tail, D : 3 * D] = jnp.where(spot, extra_kv[f : f + 1], old).astype(B16)
+    out(mixed, mixed_o)
+
+    first = lax.broadcasted_iota(jnp.int32, (PAD, 128), 1) < HEAD
+    kept = lax.broadcasted_iota(jnp.int32, (PAD, PAD), 0) < 198
+
+    def attend(f, pair):
+        here = pl.ds(pl.multiple_of(f * PAD, 16), PAD)
+        at = pl.multiple_of(pair * 128, 128)
+        q = mixed[here, pl.ds(at, 128)]
+        k = mixed[here, pl.ds(pl.multiple_of(D + at, 128), 128)]
+        v = mixed[here, pl.ds(pl.multiple_of(2 * D + at, 128), 128)]
+        total = None
+        for h in range(2):
+            mask = first if h == 0 else jnp.logical_not(first)
+            kh, vh = jnp.where(mask, k, jnp.zeros_like(k)), jnp.where(mask, v, jnp.zeros_like(v))
+            scores = jnp.where(kept, dot(kh, q, 1, 1), -1e30)
+            raised = jnp.exp(scores - jnp.max(scores, 0, keepdims=True))
+            share = (raised * (1.0 / jnp.sum(raised, 0, keepdims=True))).astype(B16)
+            shares[f * HEADS + pair * 2 + h] = share
+            part = dot(share, vh, 0, 0)
+            total = part if total is None else total + part
+        seen[here, pl.ds(at, 128)] = total.astype(B16)
+
+    def attend_frame(f):
+        def body(pair, carry):
+            attend(f, pair)
+            return carry
+        lax.fori_loop(0, 6, body, 0)
+
+    def merge_frames():
+        def body(n, carry):
+            cols = pl.ds(pl.multiple_of(n * 256, 256), 256)
+            wcols = pl.ds(pl.multiple_of(AMERGE + n * 256, 128), 256)
+            hidden[:, cols] = dot(seen[...], full[:, wcols])
+            return carry
+        lax.fori_loop(0, 3, body, 0)
+
+    def hidden_frame(f, carry):
+        here = pl.ds(pl.multiple_of(f * PAD, 16), PAD)
+        value = hidden[here, :] + xs[f].astype(F32)
+        hidden[here, :] = value
+        xh, _ = normalize(value)
+        n2[here, :] = (xh * expand_gain).astype(B16)
+        return carry
+
+    def row_mask(shape, axis):
+        index = lax.broadcasted_iota(jnp.int32, shape, axis)
+        good = index < 0
+        for f in range(4):
+            lost = jnp.where(p.dp * 4 + f < counts[0], 0, ROWS)
+            good = jnp.logical_or(good, jnp.logical_and(index >= f * PAD + lost, index < f * PAD + 197 + lost * 0))
+        return good
+
+    mask_row = jnp.where(row_mask((16, ROWS), 1), 1.0, 0.0).astype(B16)
+
+    def expand_tile(base):
+        def body(n, carry):
+            cols = pl.ds(pl.multiple_of(base + n * 256, 256), 256)
+            wcols = pl.ds(pl.multiple_of(EXPAND + base + n * 256, 128), 256)
+            grown = dot(n2[...], full[:, wcols])
+            s = 0.5 + 0.5 * jnp.tanh(0.851 * grown)
+            gated = grown * s
+            dd[:, cols] = (s + 1.702 * gated * (1.0 - s)).astype(B16)
+            gsum_o[:, cols] = dot(mask_row, gated.astype(B16))[0:8]
+            return carry
+        lax.fori_loop(0, 3, body, 0)
+
+    attend_frame(0)
+    ticks(16, 16)
+    attend_frame(1)
+    ticks(17, 17)
+    attend_frame(2)
+    attend_frame(3)
+    out(seen, seen_o)
+    out(shares, shares_o)
+    ticks(18, 18)
+    merge_frames()
+    lax.fori_loop(0, 4, hidden_frame, 0)
+    out(hidden, hidden_o)
+    expand_tile(0)
+    ticks(19, 19)
+    expand_tile(D)
+    high = hidden[...].astype(B16)
+    low = (hidden[...] - high.astype(F32)).astype(B16)
+    hsum_o[...] = (dot(mask_row, high) + dot(mask_row, low))[0:8]
+    ticks(20, 20)
+    expand_tile(2 * D)
+    ticks(21, 21)
+    out(full, full_o)
+    expand_tile(3 * D)
+    out(dd, d_o)
+    mask_col = jnp.where(row_mask((ROWS, D), 0), 1.0, 0.0)
+    n2t[...] = jnp.transpose((n2[...].astype(F32) * mask_col).astype(B16))
+    out(n2t, n2t_o)
+    normt[...] = jnp.transpose(norm[...])
+    out(normt, normt_o)
+    seent[...] = jnp.transpose(seen[...])
+    out(seent, seent_o)
+    ticks(22, 22)
+    for copy in sends:
+        copy.wait_send()
+    text_team.wait()
+    text_team.done()
+    text_hop.done()
+    for copy in outs:
+        copy.wait()
+
+
+def pack_row(row):
+    return jnp.concatenate([row[:, 128 * r : 128 * r + 128] for r in range(6)] + [jnp.zeros((2, 128), F32)], 0)
+
+
+def unpack_row(value):
+    return jnp.concatenate([value[r : r + 1] for r in range(6)], 1)
+
+
+def twice(value):
+    high = value.astype(B16)
+    return jnp.concatenate([high, (value - high.astype(F32)).astype(B16)], 0)
+
+
+def loss_kernel(
+    gsum, hsum, shrink, full, texts, counts, matches,
+    gg_o, rg_o, loss_o, shrink_grad_o, pooled_o, eg_o,
+    projection, bundle, team, gs, gr, ps, pr, rs_, rr, us, ur, team_s, team_r, hop_s, hop_r, lsem,
+):
+    p = Pos()
+    load = pltpu.make_async_copy(full.at[:, pl.ds(PROJ, 512)], projection, lsem)
+    load.start()
+    barrier(list(p.team) + p.plane())
+    bundle[:, 0:384] = jnp.concatenate([gsum[0:1, 384 * k : 384 * k + 384] for k in range(8)], 0)
+    bundle[:, 384:512] = pack_row(hsum[0:1, :])
+    hop = Team(p, bundle, team, team_s, team_r)
+    text = jnp.concatenate(
+        [jnp.concatenate([texts[i, :, r, :] for r in range(4)], 1) for i in range(4)], 0)
+    text_unit = (text * lax.rsqrt(jnp.sum(text * text, -1, keepdims=True) + 1e-06)).astype(B16)
+    hop.wait()
+    total = team[0] + team[1] + team[2] + team[3]
+    hop.done()
+    for k in range(8):
+        gs[k] = jnp.broadcast_to(total[k : k + 1, 0:384], (8, 384))
+    hop = Spread(p, gs, gr, hop_s.at[0], hop_r.at[0])
+    hop.wait()
+    gated = jnp.concatenate([gr[v][0:1] for v in range(8)], 0)
+    both = dot(twice(gated), shrink[...])
+    part = both[0:8] + both[8:16]
+    for v in range(8):
+        ps[v] = pack_row(part[v : v + 1])
+    hop.done()
+    hop = Spread(p, ps, pr, hop_s.at[1], hop_r.at[1])
+    hop.wait()
+    packed = total[:, 384:512]
+    for k in range(8):
+        packed = packed + pr[k]
+    hop.done()
+    load.wait()
+    denominator = (counts[0] * 197).astype(F32)
+    pooled = jnp.broadcast_to(unpack_row(packed / denominator), (8, D))
+    pooled_low = pooled.astype(B16)
+    embed = dot(pooled_low, projection[...])
+    rate = lax.rsqrt(jnp.sum(embed * embed, -1, keepdims=True) + 1e-06)
+    unit = embed * rate
+    logits = dot(unit.astype(B16), text_unit, 1, 1) * LOGIT_SCALE
+    peak = jnp.max(logits, -1, keepdims=True)
+    normalizer = peak + jnp.log(jnp.sum(jnp.exp(logits - peak), -1, keepdims=True))
+    matched = lax.broadcasted_iota(jnp.int32, logits.shape, 1) == matches[0]
+    loss_o[...] = jnp.broadcast_to(normalizer - jnp.sum(jnp.where(matched, logits, 0.0), -1, keepdims=True), (8, 128))
+    slope = (jnp.exp(logits - normalizer) - jnp.where(matched, 1.0, 0.0)).astype(B16)
+    unit_grad = dot(slope, text_unit) * LOGIT_SCALE
+    embed_grad = (rate * (unit_grad - unit * jnp.sum(unit * unit_grad, -1, keepdims=True))).astype(B16)
+    rg = dot(embed_grad, projection[...], 1, 1) / denominator
+    rg_o[...] = rg
+    top = lax.broadcasted_iota(jnp.int32, (16, 1), 0) == 0
+    pooled_o[...] = jnp.where(top, jnp.concatenate([pooled, pooled], 0), 0.0).astype(B16)
+    eg_o[...] = jnp.where(top, jnp.concatenate([embed_grad.astype(F32)] * 2, 0), 0.0).astype(B16)
+    rs_[...] = pack_row(rg.astype(B16).astype(F32)[0:1])
+    hop = Spread(p, rs_, rr, hop_s.at[2], hop_r.at[2], same=True)
+    hop.wait()
+    rows = jnp.concatenate([unpack_row(rr[v]) for v in range(8)], 0).astype(B16)
+    grad = dot(rows, shrink[...], 1, 1)
+    for v in range(8):
+        us[v] = jnp.broadcast_to(grad[v : v + 1], (8, 384))
+    hop.done()
+    hop = Spread(p, us, ur, hop_s.at[3], hop_r.at[3])
+    shrink_grad_o[...] = dot(twice(gated), jnp.concatenate([rows.astype(F32)] * 2, 0).astype(B16), 0, 0)
+    hop.wait()
+    for k in range(8):
+        gg_o[:, 384 * k : 384 * k + 384] = ur[k]
+    hop.done()
+
+
+def backward_kernel(
+    xs, normt_h, mixed_h, shares, seen_h, seent_h, hidden_h, n2t_h, d_h, full, gg, rg, gains, mout, counts,
+    stage, patch_o, first_o, mog_o,
+    wexp, wmerge, wheads, normt, mixed, seen, seent, hidden, n2t, dd, sbuf, hg, low, dout, lsem, psem,
+):
+    p = Pos()
+    jobs = ((n2t_h, n2t), (d_h, dd), (full.at[:, pl.ds(EXPAND, 3072)], wexp), (hidden_h, hidden),
+            (seent_h, seent), (full.at[:, pl.ds(AMERGE, D)], wmerge), (mixed_h, mixed), (seen_h, seen), (normt_h, normt),
+            (full.at[:, pl.ds(AHEADS, 3 * D)], wheads))
+    loads = []
+    for index, (source, target) in enumerate(jobs):
+        copy = pltpu.make_async_copy(source, target, lsem.at[index])
+        copy.start()
+        loads.append(copy)
+    attend_gain, expand_gain = gains[1:2, :], gains[2:3, :]
+    loads[0].wait()
+    loads[1].wait()
+
+    def expand_tile(n, carry):
+        cols = pl.ds(pl.multiple_of(n * 256, 256), 256)
+        tile = dd[:, cols]
+        scale = gg[0:1, cols]
+        stage[:, :, cols] = (dot(n2t[...], tile) * scale).astype(B16).reshape(8, 96, 256)
+        dd[:, cols] = (tile.astype(F32) * scale).astype(B16)
+        return carry
+
+    lax.fori_loop(0, 12, expand_tile, 0)
+    loads[2].wait()
+
+    def norm_tile(n, carry):
+        cols = pl.ds(pl.multiple_of(n * 256, 256), 256)
+        hg[:, cols] = dot(dd[...], wexp[cols, :], 1, 1)
+        return carry
+
+    lax.fori_loop(0, 3, norm_tile, 0)
+    loads[3].wait()
+
+    def hidden_frame(f, total):
+        here = pl.ds(pl.multiple_of(f * PAD, 16), PAD)
+        limit = jnp.where(p.dp * 4 + f < counts[0], 197, 0)
+        good = lax.broadcasted_iota(jnp.int32, (PAD, D), 0) < limit
+        xh, rate = normalize(hidden[here, :])
+        dy = jnp.where(good, hg[here, :], 0.0)
+        e = dy * expand_gain
+        grad = rate * (e - jnp.mean(e, -1, keepdims=True) - xh * jnp.mean(e * xh, -1, keepdims=True))
+        grad = grad + jnp.where(good, rg[0:1, :], 0.0)
+        hg[here, :] = grad
+        low[here, :] = grad.astype(B16)
+        return total + jnp.sum(dy * xh, 0, keepdims=True)
+
+    expand_gain_grad = lax.fori_loop(0, 4, hidden_frame, jnp.zeros((1, D), F32))
+    loads[4].wait()
+    loads[5].wait()
+
+    def merge_tile(n, carry):
+        cols = pl.ds(pl.multiple_of(n * 256, 256), 256)
+        stage[:, :, pl.ds(pl.multiple_of(3072 + n * 256, 128), 256)] = dot(seent[...], low[:, cols]).astype(B16).reshape(8, 96, 256)
+        dout[:, cols] = dot(low[...], wmerge[cols, :], 1, 1).astype(B16)
+        return carry
+
+    lax.fori_loop(0, 3, merge_tile, 0)
+    loads[6].wait()
+    loads[7].wait()
+    first = lax.broadcasted_iota(jnp.int32, (PAD, 128), 1) < HEAD
+
+    def fetch(index, slot):
+        return pltpu.make_async_copy(shares.at[pl.ds(index * 2, 2)], sbuf.at[slot], psem.at[slot])
+
+    fetch(0, 0).start()
+
+    def attend(index, carry):
+        f, pair = index // 6, lax.rem(index, 6)
+        slot = lax.rem(index, 2)
+
+        @pl.when(index < 23)
+        def _():
+            fetch(index + 1, 1 - slot).start()
+
+        fetch(index, slot).wait()
+        here = pl.ds(pl.multiple_of(f * PAD, 16), PAD)
+        at = pl.multiple_of(pair * 128, 128)
+        qs, ks, vs = (pl.ds(pl.multiple_of(b + at, 128), 128) for b in (0, D, 2 * D))
+        q, k, v = mixed[here, qs], mixed[here, ks], mixed[here, vs]
+        do, o = dout[here, qs], seen[here, qs]
+        right = jnp.concatenate([do, (-(do.astype(F32) * o.astype(F32))).astype(B16)], 1)
+        dq = dk = dv = None
+        zero = jnp.zeros_like(q)
+        for h in range(2):
+            mask = first if h == 0 else jnp.logical_not(first)
+            share = sbuf[slot, h]
+            left = jnp.concatenate([jnp.where(mask, v, zero), jnp.where(mask, jnp.ones_like(v), zero)], 1)
+            ds = (share.astype(F32) * dot(left, right, 1, 1)).astype(B16)
+            pq = dot(ds, jnp.where(mask, k, zero), 0, 0)
+            pk = dot(ds, jnp.where(mask, q, zero))
+            pv = dot(share, jnp.where(mask, do, zero))
+            dq, dk, dv = (pq, pk, pv) if h == 0 else (dq + pq, dk + pk, dv + pv)
+        mixed[here, qs] = (dq * HEAD ** (-0.5)).astype(B16)
+        mixed[here, ks] = dk.astype(B16)
+        mixed[here, vs] = dv.astype(B16)
+        return carry
+
+    lax.fori_loop(0, 24, attend, 0)
+    loads[8].wait()
+
+    def heads_tile(n, carry):
+        cols = pl.ds(pl.multiple_of(n * 256, 256), 256)
+        stage[:, :, pl.ds(pl.multiple_of(3840 + n * 256, 128), 256)] = dot(normt[...], mixed[:, cols]).astype(B16).reshape(8, 96, 256)
+        return carry
+
+    lax.fori_loop(0, 9, heads_tile, 0)
+    loads[9].wait()
+
+    def tokens_tile(n, carry):
+        cols = pl.ds(pl.multiple_of(n * 256, 256), 256)
+        hidden[:, cols] = dot(mixed[...], wheads[cols, :], 1, 1)
+        return carry
+
+    lax.fori_loop(0, 3, tokens_tile, 0)
+    attend_gain_grad = jnp.zeros((1, D), F32)
+    firsts, messages = [], []
+    spot = lax.broadcasted_iota(jnp.int32, (PAD, 1), 0) == 197
+    for f in range(4):
+        here = pl.ds(f * PAD, PAD)
+        xh, rate = normalize(jnp.where(spot, mout[f : f + 1, :], xs[f].astype(F32)))
+        dy = hidden[here, :]
+        e = dy * attend_gain
+        grad = rate * (e - jnp.mean(e, -1, keepdims=True) - xh * jnp.mean(e * xh, -1, keepdims=True))
+        attend_gain_grad = attend_gain_grad + jnp.sum(dy * xh, 0, keepdims=True)
+        patch = hg[here, :] + grad
+        patch_o[f] = patch.astype(B16)
+        firsts.append(patch[0:1])
+        messages.append(grad[197:198])
+    first_o[...] = jnp.concatenate(firsts + [jnp.zeros((4, D), F32)], 0)
+    mog_o[...] = jnp.concatenate(messages + [jnp.zeros((4, D), F32)], 0)
+    tall = jnp.concatenate([attend_gain_grad, expand_gain_grad, jnp.zeros((126, D), F32)], 0)
+    stage[:, :, 6144:6272] = jnp.transpose(tall).astype(B16).reshape(8, 96, 128)
+
+
+RJOBS = ((0, 768), (768, 768), (1536, 768), (2304, 768), (3072, 768), (3840, 768), (4608, 768), (5376, 896))
+BUNDLE = 8448
+SIXTH = BUNDLE // 6
+
+
+def reduce_kernel(
+    stage_h, mog, first, full, leaders, message, mnorm, mmix, mshare, told, pooled, eg, gains,
+    out, courier_o, cheads_o, cmerge_o, proj_o, cgain_o, lead_o,
+    stage, rc, rx, ry, rz, own, rf, fin, rcf, bundle, team, weights, s_r, r_r, s_b, r_b, team_s, team_r, lsem,
+):
+    p = Pos()
+    loads = []
+    for index, (first_col, count, target) in enumerate(((CMERGE, D, 3072), (CHEADS, 3 * D, D), (COURIER, D, 0))):
+        loads.append(pltpu.make_async_copy(full.at[:, pl.ds(first_col, count)], weights.at[:, pl.ds(target, count)], lsem.at[index]))
+        loads[-1].start()
+    big = pltpu.make_async_copy(stage_h, stage, lsem.at[3])
+    big.start()
+    barrier(p.peers() + [p.cross])
+    hop = Team(p, mog, team, team_s, team_r)
+    big.wait()
+    reduce = Reduce(p, stage, (rc, rx, ry, rz, own, rf, fin, rcf), out, RJOBS, s_r, r_r)
+    lag = (0, 1, 2, 3, 4, 5, 6, 7)
+    reduce.tick(0, lag)
+    reduce.tick(1, lag)
+    hop.wait()
+    out_grad = jnp.concatenate([team[i][0:4] for i in range(4)], 0)
+    for load in loads:
+        load.wait()
+    courier_gain = gains[0:1, :]
+    mq, mk, mv = mmix[:, 0:D], mmix[:, D : 2 * D], mmix[:, 2 * D : 3 * D]
+    out_low = out_grad.astype(B16)
+    told_grad = dot(out_low, weights[:, 3072:3840], 1, 1).astype(B16)
+    upstream = spread_heads(told_grad)
+    share = mshare[...]
+    share_grad = dot(upstream, mv, 1, 1)
+    dv = dot(share.astype(B16), upstream, 0, 0)
+    inner = jnp.sum(share * share_grad, -1, keepdims=True)
+    ds = (share * (share_grad - inner)).astype(B16)
+    dq = join_heads(dot(ds, mk)) * HEAD ** (-0.5)
+    dk = dot(ds, spread_heads(mq), 0, 0) * HEAD ** (-0.5)
+    mixed_grad = jnp.concatenate([dq, dk, dv], 1).astype(B16)
+    norm_grad = dot(mixed_grad, weights[:, D : 4 * D], 1, 1)
+    xh, rate = normalize(message[...])
+    e = norm_grad * courier_gain
+    grad = rate * (e - jnp.mean(e, -1, keepdims=True) - xh * jnp.mean(e * xh, -1, keepdims=True))
+    message_grad = (out_grad + grad).astype(B16)
+    leader_grad = dot(message_grad, weights[:, 0:D], 1, 1)
+    lead_o[...] = jnp.concatenate([row_of(leader_grad, p.dp * 4 + f) for f in range(4)] + [jnp.zeros((4, D), F32)], 0) + first[...]
+    parts = (message_grad, mixed_grad, out_low, leaders[...], mnorm[...], told[...], pooled[...], eg[...],
+             (norm_grad * xh).astype(B16))
+    col = 0
+    for part in parts:
+        bundle[p.k, :, col : col + part.shape[1]] = part
+        col += part.shape[1]
+
+    def block(k, start, count, job):
+        return bundle.at[k, :, pl.ds(pl.multiple_of(start * SIXTH, 128), count * SIXTH)]
+
+    gather = Gather(p, block, 1, s_b, r_b)
+    for t in range(2, 8):
+        gather.stage(t - 2, 0)
+        reduce.tick(t, lag)
+    whole = bundle[...].reshape(128, BUNDLE)
+    pick = jnp.where(
+        jnp.logical_and(lax.broadcasted_iota(jnp.int32, (D, 128), 0) == p.k * 96 + lax.broadcasted_iota(jnp.int32, (D, 128), 1),
+                        lax.broadcasted_iota(jnp.int32, (D, 128), 1) < 96), 1.0, 0.0).astype(B16)
+
+    def product(left, width, right, columns):
+        chosen = dot(whole[:, left : left + width], pick).astype(B16)
+        return dot(chosen, whole[:, right : right + columns], 0, 0)[0:96]
+
+    courier_o[...] = product(3840, D, 0, D)
+    cheads_o[...] = product(4608, D, D, 3 * D)
+    cmerge_o[...] = product(5376, D, 3072, D)
+    proj_o[...] = product(6144, D, 6912, 512)
+    gain_grad = jnp.sum(whole[:, 7424:8192].astype(F32), 0, keepdims=True)
+    gain_grad = twice(jnp.broadcast_to(gain_grad, (8, D)))
+    both = dot(pick, gain_grad, 0, 1)
+    cgain_o[...] = both[0:96, 0:8] + both[0:96, 8:16]
+    for t in range(8, len(RJOBS) + 7):
+        reduce.tick(t, lag)
+    hop.done()
+
+
+def any_spec():
+    return pl.BlockSpec(memory_space=pl.ANY)
+
+
+def vmem_spec():
+    return pl.BlockSpec(memory_space=pltpu.VMEM)
+
+
+def smem_spec():
+    return pl.BlockSpec(memory_space=pltpu.SMEM)
+
+
+def sds(shape, dtype):
+    return jax.ShapeDtypeStruct(shape, dtype)
+
+
+def dma(*shape):
+    return pltpu.SemaphoreType.DMA(shape)
+
+
+def vm(shape, dtype):
+    return pltpu.VMEM(shape, dtype)
+
+
+def fast(
+    patches, counts, captions, matches, courier, courier_gain, courier_heads, courier_merge, attend_gain, attend_heads,
+    attend_merge, expand_gain, expand_weight, shrink_weight, projection,
+):
+    caption = jnp.pad(captions.astype(F32).reshape(4, 128), ((0, 4), (0, 0)))
+    xs = jnp.pad(patches[0], ((0, 0), (0, PAD - 197), (0, 0)))
+    lead = jnp.pad(patches[0, :, 0, :].astype(F32), ((0, 4), (0, 0)))
+    gain_block = jnp.stack([courier_gain, attend_gain, expand_gain], 1)
+    gain_block = jnp.pad(gain_block, ((0, 0), (0, 125)))
+    anys, vmem, smem = any_spec(), vmem_spec(), smem_spec()
+    (full, normt, mixed, shares, seen, seent, hidden, n2t, dd, gsum, hsum, gains,
+     leaders, message, mnorm, mmix, mshare, told, mout, texts) = pl.pallas_call(
+        forward_kernel,
+        out_shape=(
+            sds((D, NCOLS), B16), sds((D, ROWS), B16), sds((ROWS, 3 * D), B16), sds((48, PAD, PAD), B16), sds((ROWS, D), B16),
+            sds((D, ROWS), B16), sds((ROWS, D), F32), sds((D, ROWS), B16), sds((ROWS, 4 * D), B16), sds((8, 4 * D), F32),
+            sds((8, D), F32), sds((8, D), F32), sds((16, D), B16), sds((16, D), F32), sds((16, D), B16), sds((16, 3 * D), B16),
+            sds((192, 16), F32), sds((16, D), B16), sds((8, D), F32), sds((4, 8, 8, 128), F32)),
+        in_specs=[vmem, vmem, vmem, smem] + [anys] * 8,
+        out_specs=tuple([anys] * 9 + [vmem] * 11),
+        scratch_shapes=[
+            vm((D, NCOLS), B16), vm((4, 8, D), F32), vm((ROWS, D), B16), vm((D, ROWS), B16), vm((ROWS, 3 * D), B16),
+            vm((48, PAD, PAD), B16), vm((ROWS, D), B16), vm((D, ROWS), B16), vm((ROWS, D), F32), vm((ROWS, D), B16),
+            vm((D, ROWS), B16), vm((ROWS, 4 * D), B16),
+            vm((8, 8, 128), F32), dma(len(JOBS), 28), dma(len(JOBS), 28), dma(8), dma(2, 3), dma(2, 3), dma(7), dma(7), dma(9)],
+        compiler_params=pltpu.CompilerParams(collective_id=0, has_side_effects=True, vmem_limit_bytes=60 << 20),
+        name="forward",
+    )(xs, lead, caption, counts, courier, gain_block, courier_heads, attend_heads, courier_merge, attend_merge, expand_weight, projection)
+    gg, rg, loss, shrink_grad, pooled, eg = pl.pallas_call(
+        loss_kernel,
+        out_shape=(sds((8, 4 * D), F32), sds((8, D), F32), sds((8, 128), F32), sds((384, D), F32), sds((16, D), B16),
+                   sds((16, 512), B16)),
+        in_specs=[vmem, vmem, vmem, anys, vmem, smem, smem],
+        out_specs=tuple([vmem] * 6),
+        scratch_shapes=[
+            vm((D, 512), B16), vm((8, 512), F32), vm((4, 8, 512), F32), vm((8, 8, 384), F32), vm((8, 8, 384), F32),
+            vm((8, 8, 128), F32), vm((8, 8, 128), F32), vm((8, 128), F32), vm((8, 8, 128), F32), vm((8, 8, 384), F32),
+            vm((8, 8, 384), F32), dma(3), dma(3), dma(4, 7), dma(4, 7), pltpu.SemaphoreType.DMA],
+        compiler_params=pltpu.CompilerParams(collective_id=1, has_side_effects=True, vmem_limit_bytes=60 << 20),
+        name="loss",
+    )(gsum, hsum, shrink_weight, full, texts, counts, matches)
+    stage, patch, first, mog = pl.pallas_call(
+        backward_kernel,
+        out_shape=(sds((8, 96, 6272), B16), sds((4, PAD, D), B16), sds((8, D), F32), sds((8, D), F32)),
+        in_specs=[vmem, anys, anys, anys, anys, anys, anys, anys, anys, anys, vmem, vmem, vmem, vmem, smem],
+        out_specs=tuple([vmem] * 4),
+        scratch_shapes=[
+            vm((D, 4 * D), B16), vm((D, D), B16), vm((D, 3 * D), B16), vm((D, ROWS), B16), vm((ROWS, 3 * D), B16),
+            vm((ROWS, D), B16), vm((D, ROWS), B16), vm((ROWS, D), F32), vm((D, ROWS), B16), vm((ROWS, 4 * D), B16),
+            vm((2, 2, PAD, PAD), B16), vm((ROWS, D), F32), vm((ROWS, D), B16), vm((ROWS, D), B16), dma(10), dma(2)],
+        compiler_params=pltpu.CompilerParams(vmem_limit_bytes=60 << 20),
+        name="backward",
+    )(xs, normt, mixed, shares, seen, seent, hidden, n2t, dd, full, gg, rg, gains, mout, counts)
+    out, courier_grad, cheads_grad, cmerge_grad, proj_grad, cgain, leads = pl.pallas_call(
+        reduce_kernel,
+        out_shape=(sds((96, 6272), F32), sds((96, D), F32), sds((96, 3 * D), F32), sds((96, D), F32), sds((96, 512), F32),
+                   sds((96, 8), F32), sds((8, D), F32)),
+        in_specs=[anys, vmem, vmem, anys] + [vmem] * 9,
+        out_specs=tuple([vmem] * 7),
+        scratch_shapes=[
+            vm((8, 96, 6272), B16), vm((8, 48, 6272), B16), vm((8, 16, 6272), B16), vm((4, 32, 6272), B16),
+            vm((3, 32, 6272), B16), vm((32, 6272), B16), vm((32, 6272), B16), vm((96, 6272), B16), vm((48, 6272), B16),
+            vm((8, 16, BUNDLE), B16), vm((4, 8, D), F32), vm((D, 5 * D), B16),
+            dma(len(RJOBS), 11), dma(len(RJOBS), 11), dma(1, 28), dma(1, 28), dma(3), dma(3), dma(4)],
+        compiler_params=pltpu.CompilerParams(collective_id=2, has_side_effects=True, vmem_limit_bytes=60 << 20),
+        name="reduce",
+    )(stage, mog, first, full, leaders, message, mnorm, mmix, mshare, told, pooled, eg, gains)
+    patch_grad = jnp.concatenate([leads[0:4, None, :].astype(B16), patch[:, 1:197]], 1)[None]
+    return (
+        loss[0:1, 0], patch_grad, courier_grad, cgain[:, 0], cheads_grad, cmerge_grad, out[:, 6144], out[:, 3840:6144],
+        out[:, 3072:3840], out[:, 6145], out[:, 0:3072], shrink_grad, proj_grad,
+    )
 
 
 def joined_2(value, axis, join):
@@ -406,8 +1296,9 @@
 
 
 def solution(mesh):
+    fitting = mesh.shape['dp'] == 4 and mesh.shape['fsdp'] == Z * Y
     return jax.shard_map(
-        shards,
+        fast if fitting else shards,
         mesh=mesh,
         in_specs=(
             P("fsdp", "dp", None, None),

time: 1510 us -> 300 us (0.20)
  waiting for transfers between devices: 998 us -> 0 us
  Pallas kernels: 0 us -> 278 us
  blocking collectives: 155 us -> 0 us
  matrix products: 143 us -> 0 us
  other arithmetic: 90.5 us -> 1.54 us
  local copies, waits for them, and re-layouts: 73.2 us -> 17.4 us
  between operations: 24.5 us -> 2.08 us
  loops' own time: 18.3 us -> 0 us
    reduce_scatter x7 -> x0, waiting for transfers between devices: 679 us -> none  [the longest x1 164 us: shards(): lax.psum_scatter(block_grads[5], 'fsdp', scatter_dimension=0, tiled=True)]
    pallas_call x0 -> x4, Pallas kernels: none -> 278 us  [the longest x1 112 us: fast(): pl.pallas_call(forward_kernel, out_shape=(sds((D, NCOLS), B16), sds((D, R...]
    all_gather x7 -> x0, waiting for transfers between devices: 242 us -> none  [the longest x1 71.3 us: fetch(): lax.all_gather(shrink_weight, 'fsdp', axis=0, tiled=True)]
    dot_general x55 -> x0, matrix products: 143 us -> none  [the longest x2 14.8 us: frame_backward(): jnp.einsum('bpd,bpm->dm', normed_two, grown_grad, preferred_element_type=...]
    unnamed x17 -> x0, waiting for transfers between devices: 76.7 us -> none
    all_gather x4 -> x0, blocking collectives: 71.5 us -> none  [the longest x1 34.5 us: shards(): lax.all_gather(projection, 'fsdp', axis=0, tiled=True)]
    unnamed x3 -> x0, blocking collectives: 66.2 us -> none
    reduce_sum x22 -> x0, other arithmetic: 41.9 us -> none  [the longest x7 17.6 us: layer_norm(): center = value - jnp.mean(value, -1, keepdims=True)]
  transfers between devices with their start and end apart: 16 -> 0, of which waited for: 13 -> 0; matrix products, arithmetic and copies ran while one was open for 14% -> 0% of each run, Pallas kernels for 0% -> 0%
where the time goes in v1:
time: 300 us; the launch traced here: 299 us
  Pallas kernels  278 us (93%)
  local copies, waits for them, and re-layouts  17.4 us (6%)
    pallas_call x1, Pallas kernels, fast(): pl.pallas_call(forward_kernel, out_shape=(sds((D, NCOLS), B16), sds((D, R...  112 us
    pallas_call x1, Pallas kernels, fast(): pl.pallas_call(reduce_kernel, out_shape=(sds((96, 6272), F32), sds((96, D...  79.9 us
    pallas_call x1, Pallas kernels, fast(): pl.pallas_call(backward_kernel, out_shape=(sds((8, 96, 6272), B16), sds((...  56 us
    pallas_call x1, Pallas kernels, fast(): pl.pallas_call(loss_kernel, out_shape=(sds((8, 4 * D), F32), sds((8, D),...  30 us
    unnamed x29, local copies, waits for them, and re-layouts  7.7 us

profile of v1, /device:TPU:0, one launch (start us, length us, event | category | flops | bytes accessed | tf_op | source)
XLA Modules:
  0.0 298.7 jit_solution(3540417818347386587)
XLA Ops:
  0.6 1.4 copy.45
  2.1 0.0 copy-start.7
  2.1 0.0 copy-start.8
  2.1 0.0 copy-start.9
  2.1 0.0 copy-start.10
  2.1 1.2 pad.20.xs
  3.3 0.7 slice_bitcast_fusion
  4.0 0.6 pad_convert_fusion.lead
  4.6 0.0 copy-done.7
  4.6 0.6 pad_convert_fusion.1.caption
  5.9 0.0 copy-done.8
  5.9 0.0 copy-done.9
  5.9 0.0 copy-done.10
  5.9 0.1 copy.41
  6.0 0.6 pad.25.gains
  6.6 111.8 %forward.1 = (bf16[768,10624]{1,0:T(8,128)(2,1)}, bf16[768,832]{1,0:T(8,128)(2,1)}, bf16[832,2304]{1,0:T(8,128)(2,1)}, bf16[48,208,208]{2,1,0:T(8,128)(2,1)}, bf...) custom-call(bf16[4,208,768]{2,1,0:T(8,128)(2,1)} %pad.20.xs, ...), custom_call_target="tpu_custom_call" | custom-call | tf_op jit(solution)/shard_map/forward/pallas_call | solution.py:842
  119.1 30.0 %loss.1 = (f32[8,3072]{1,0:T(8,128)}, f32[8,768]{1,0:T(8,128)}, f32[8,128]{1,0:T(8,128)}, f32[384,768]{1,0:T(8,128)}, bf16[16,768]{1,0:T(8,128)(2,1)}, /*index=5*/bf16[16,512]{1,0:T(8,128)(2,1)}) custom-call(f32[8,3072]{1,0:T(8,128)} %get-tuple-element.50.gsum, f32[8,768]{1,0:T(8,128)} %get-tuple-element.51.hsum, bf16[384,768]{1,0:T(8,128)(2,1)} %shrink.1, ...), custom_call_target="tpu_custom_call" | custom-call | tf_op jit(solution)/shard_map/loss/pallas_call | solution.py:859
  149.1 1.2 slice.32
  150.3 56.0 %backward.1 = (bf16[8,96,6272]{2,1,0:T(8,128)(2,1)}, bf16[4,208,768]{2,1,0:T(8,128)(2,1)}, f32[8,768]{1,0:T(8,128)}, f32[8,768]{1,0:T(8,128)}) custom-call(bf16[4,208,768]{2,1,0:T(8,128)(2,1)} %pad.20.xs, bf16[768,832]{1,0:T(8,128)(2,1)} %get-tuple-element.55.normt_h, bf16[832,2304]{1,0:T(8,128)(2,1)} %get-tuple-element.56.mixed_h, ...), custom_call_target="tpu_custom_call" | custom-call | tf_op jit(solution)/shard_map/backward/pallas_call | solution.py:872
  206.3 1.6 slice.34
  207.9 79.9 %reduce.8 = (f32[96,6272]{1,0:T(8,128)}, f32[96,768]{1,0:T(8,128)}, f32[96,2304]{1,0:T(8,128)}, f32[96,768]{1,0:T(8,128)}, f32[96,512]{1,0:T(8,128)}, /*index=5*/f32[96,8]{1,0:T(8,128)}, f32[8,768]{1,0:T(8,128)}) custom-call(bf16[8,96,6272]{2,1,0:T(8,128)(2,1)} %get-tuple-element.67.stage_h, f32[8,768]{1,0:T(8,128)} %get-tuple-element.68.mog, ...), custom_call_target="tpu_custom_call" | custom-call | tf_op jit(solution)/shard_map/reduce/pallas_call | solution.py:884
  287.8 0.7 fusion
  288.5 0.0 copy-start.6
  288.6 0.3 maximum_bitcast_fusion
  288.9 0.0 copy-start
  288.9 1.5 copy.43
  290.4 0.0 copy-done.6
  290.4 0.6 copy-done
  291.0 0.7 slice_reduce_fusion
  291.7 1.0 slice.37
  292.7 0.7 slice.38
  293.4 0.0 copy-start.4
  293.4 0.0 copy-start.2
  293.4 1.1 slice.40
  294.5 0.0 copy-start.3
  294.5 0.0 copy-done.4
  294.5 0.7 copy.53
  295.3 0.0 copy-done.2
  295.3 0.0 copy-start.1
  295.3 0.9 copy.54
  296.2 0.0 copy-done.3
  296.2 0.7 copy.55
  296.9 0.0 copy-done.1
  296.9 0.0 copy-start.5
  296.9 1.0 copy.56
  297.9 0.1 copy-done.5
  298.0 0.7 copy.57
  (3 shorter events, 0.0 us)
Async XLA Ops:
  2.1 2.5 copy-start.7
  2.1 3.8 %copy-start.8 = (bf16[96]{0:T(256)(128)(2,1)S(1)}, bf16[96]{0:T(256)(128)(2,1)}, u32[]{:S(2)}) copy-start(bf16[96]{0:T(256)(128)(2,1)} %param.26) | copy-start | bytes 580
  2.1 3.8 %copy-start.9 = (bf16[96]{0:T(256)(128)(2,1)S(1)}, bf16[96]{0:T(256)(128)(2,1)}, u32[]{:S(2)}) copy-start(bf16[96]{0:T(256)(128)(2,1)} %param.23) | copy-start | bytes 580
  2.1 3.8 %copy-start.10 = (bf16[96]{0:T(256)(128)(2,1)S(1)}, bf16[96]{0:T(256)(128)(2,1)}, u32[]{:S(2)}) copy-start(bf16[96]{0:T(256)(128)(2,1)} %param.20) | copy-start | bytes 580
  288.5 1.8 copy-start.6
  288.9 2.1 copy-start
  293.4 1.1 copy-start.4
  293.4 1.8 copy-start.2
  294.5 1.6 copy-start.3
  295.3 1.6 copy-start.1
  296.9 1.1 copy-start.5

commit v2 on v1

--- a/solution.py
+++ b/solution.py
@@ -168,9 +168,10 @@
 
 
 class Reduce:
-    def __init__(self, p, stage, buffers, out, jobs, send, receive):
-        self.p, self.stage, self.out, self.jobs, self.send, self.receive = p, stage, out, jobs, send, receive
-        self.rc, self.rx, self.ry, self.rz, self.own, self.rf, self.fin, self.rcf = buffers
+    def __init__(self, p, stage, buffers, fin, jobs, send, receive):
+        self.p, self.stage, self.fin, self.jobs, self.send, self.receive = p, stage, fin, jobs, send, receive
+        self.rc, self.rx, self.ry, self.rz, self.own, self.rf = buffers
+        self.at = [0] * len(jobs)
 
     def copies(self, job, step):
         p = self.p
@@ -181,7 +182,8 @@
         away = pl.ds(pl.multiple_of((3 * p.c + 2 * (1 - p.x)) * 16, 16), 16)
         s, r = self.send, self.receive
         if step == 0:
-            return [remote(self.stage.at[:, other, cols], self.rc.at[:, :, cols], s.at[job, 0], r.at[job, 0], p.core)]
+            target = self.rc.at[job % 4, :, :, pl.ds(0, count)]
+            return [remote(self.stage.at[:, other, cols], target, s.at[job, 0], r.at[job, 0], p.core)]
         if step == 1:
             return [remote(self.stage.at[:, away, cols], self.rx.at[:, :, cols], s.at[job, 1], r.at[job, 1], p.xp)]
         if step == 2:
@@ -192,32 +194,51 @@
                            r.at[job, 6 + d], device) for d, device in enumerate(p.column())]
         if step == 4:
             return [remote(self.own.at[:, cols], self.rf.at[:, cols], s.at[job, 9], r.at[job, 9], p.xp)]
-        return [remote(self.fin.at[half, cols], self.rcf.at[:, cols], s.at[job, 10], r.at[job, 10], p.core)]
-
-    def step(self, step, job):
-        if job < 0 or job >= len(self.jobs):
-            return
+        return [remote(self.fin.at[half, cols], self.fin.at[half, cols], s.at[job, 10], r.at[job, 10], p.core)]
+
+    def next(self, *jobs, scale=None):
+        for job in jobs:
+            self.step(self.at[job], job, scale)
+            self.at[job] += 1
+
+    def step(self, step, job, scale):
         p = self.p
         first, count = self.jobs[job]
         cols = pl.ds(first, count)
-        if step > 0 and step < 7:
+        half, other = pl.ds(pl.multiple_of(48 * p.c, 16), 48), pl.ds(pl.multiple_of(48 * (1 - p.c), 16), 48)
+        carried = pl.ds(pl.multiple_of((3 * p.c + p.x) * 16, 16), 32)
+        if step == 6:
+            remote(self.fin.at[other, cols], self.fin.at[other, cols], self.send.at[job, 10], self.receive.at[job, 10],
+                   p.core).wait_recv()
+        elif step > 0 and step < 6:
             for copy in self.copies(job, step - 1):
                 copy.wait_recv()
         if step == 1:
-            half = pl.ds(pl.multiple_of(48 * p.c, 16), 48)
-            for k in range(Z * Y):
-                self.stage[k, half, cols] = (self.stage[k, half, cols].astype(F32) + self.rc[k, :, cols].astype(F32)).astype(B16)
+            def add(k, carry):
+                value = self.stage[k, half, cols].astype(F32) + self.rc[job % 4, k, :, pl.ds(0, count)].astype(F32)
+                self.stage[k, half, cols] = value.astype(B16)
+                return carry
+            lax.fori_loop(0, Z * Y, add, 0)
         elif step == 2:
-            single = pl.ds(pl.multiple_of((3 * p.c + 2 * p.x) * 16, 16), 16)
-            for k in range(Z * Y):
-                self.stage[k, single, cols] = (self.stage[k, single, cols].astype(F32) + self.rx[k, :, cols].astype(F32)).astype(B16)
+            def add(k, carry):
+                value = self.stage[k, carried, cols].astype(F32)
+                other_x = self.rx[k, :, cols].astype(F32)
+                top = value[0:16] + jnp.where(p.x == 0, other_x, 0.0)
+                low = value[16:32] + jnp.where(p.x == 0, 0.0, other_x)
+                value = jnp.concatenate([top, low], 0)
+                if scale is not None:
+                    value = value * scale[0:1, cols]
+                self.stage[k, carried, cols] = value.astype(B16)
+                return carry
+            lax.fori_loop(0, Z * Y, add, 0)
         elif step == 3:
-            carried = pl.ds(pl.multiple_of((3 * p.c + p.x) * 16, 16), 32)
-            for z in range(Z):
+            def add(z, carry):
                 k = z * Y + p.y
-                self.stage[k, carried, cols] = (self.stage[k, carried, cols].astype(F32) + self.ry[z, :, cols].astype(F32)).astype(B16)
+                value = self.stage[k, carried, cols].astype(F32) + self.ry[z, :, cols].astype(F32)
+                self.stage[k, carried, cols] = value.astype(B16)
+                return carry
+            lax.fori_loop(0, Z, add, 0)
         elif step == 4:
-            carried = pl.ds(pl.multiple_of((3 * p.c + p.x) * 16, 16), 32)
             total = self.stage[p.k, carried, cols].astype(F32)
             for d in range(3):
                 total = total + self.rz[d, :, cols].astype(F32)
@@ -227,13 +248,7 @@
             left = jnp.where(p.x == 0, mine[0:16], theirs[0:16])
             right = jnp.where(p.x == 0, theirs[16:32], mine[16:32])
             middle = jnp.where(p.x == 0, mine[16:32], mine[0:16]) + jnp.where(p.x == 0, theirs[0:16], theirs[16:32])
-            half = pl.ds(pl.multiple_of(48 * p.c, 16), 48)
             self.fin[half, cols] = jnp.concatenate([left, middle, right], 0).astype(B16)
-        elif step == 6:
-            other = pl.ds(pl.multiple_of(48 * (1 - p.c), 16), 48)
-            half = pl.ds(pl.multiple_of(48 * p.c, 16), 48)
-            self.out[half, cols] = self.fin[half, cols].astype(F32)
-            self.out[other, cols] = self.rcf[:, cols].astype(F32)
         if step < 6:
             for copy in self.copies(job, step):
                 copy.start()
@@ -241,10 +256,6 @@
             for earlier in range(6):
                 for copy in self.copies(job, earlier):
                     copy.wait_send()
-
-    def tick(self, t, lag):
-        for step in (7, 6, 5, 4, 3, 2, 1, 0):
-            self.step(step, t - lag[step])
 
 
 def dot(a, b, ca=1, cb=0):
@@ -512,27 +523,58 @@
     return jnp.concatenate([high, (value - high.astype(F32)).astype(B16)], 0)
 
 
-def loss_kernel(
-    gsum, hsum, shrink, full, texts, counts, matches,
-    gg_o, rg_o, loss_o, shrink_grad_o, pooled_o, eg_o,
-    projection, bundle, team, gs, gr, ps, pr, rs_, rr, us, ur, team_s, team_r, hop_s, hop_r, lsem,
+RJOBS = ((0, 768), (768, 768), (1536, 768), (2304, 768), (3072, 768), (3840, 768), (4608, 768), (5376, 768), (6144, 128))
+BUNDLE = 8448
+SIXTH = BUNDLE // 6
+
+
+def rear_kernel(
+    xs_h, normt_h, mixed_h, shares, seen_h, seent_h, hidden_h, n2t_h, d_h, full,
+    gsum, hsum, shrink, texts, gains, mout, leaders, message, mnorm, mmix, mshare, told, counts, matches,
+    patch_h, fin, loss_o, shrink_grad_o, courier_o, cheads_o, cmerge_o, proj_o, cgain_o, lead_o,
+    stage, rc, rx, ry, rz, own, rf, bundle, wx, wmerge, wheads, normt, mixed, seen, seent, hidden, n2t, dd, sbuf, hg, low, dout,
+    projection, vecs, team, gs, gr, ps, pr, rs_, rr, us, ur, gg, first, mog, mog_team,
+    s_r, r_r, s_b, r_b, team_s, team_r, hop_s, hop_r, lsem, psem,
 ):
     p = Pos()
-    load = pltpu.make_async_copy(full.at[:, pl.ds(PROJ, 512)], projection, lsem)
-    load.start()
-    barrier(list(p.team) + p.plane())
-    bundle[:, 0:384] = jnp.concatenate([gsum[0:1, 384 * k : 384 * k + 384] for k in range(8)], 0)
-    bundle[:, 384:512] = pack_row(hsum[0:1, :])
-    hop = Team(p, bundle, team, team_s, team_r)
-    text = jnp.concatenate(
-        [jnp.concatenate([texts[i, :, r, :] for r in range(4)], 1) for i in range(4)], 0)
+    pending = ((n2t_h, n2t), (d_h, dd), (full.at[:, pl.ds(PROJ, 512)], projection), (full.at[:, pl.ds(EXPAND, 3072)], wx),
+               (hidden_h, hidden), (seent_h, seent), (full.at[:, pl.ds(AMERGE, D)], wmerge), (mixed_h, mixed), (seen_h, seen),
+               (normt_h, normt), (full.at[:, pl.ds(AHEADS, 3 * D)], wheads))
+    loads = []
+
+    def load(source, target):
+        copy = pltpu.make_async_copy(source, target, lsem.at[len(loads)])
+        copy.start()
+        loads.append(copy)
+        return copy
+
+    for source, target in pending:
+        load(source, target)
+    barrier(p.plane() + list(p.team))
+    vecs[:, 0:384] = jnp.concatenate([gsum[0:1, 384 * k : 384 * k + 384] for k in range(8)], 0)
+    vecs[:, 384:512] = pack_row(hsum[0:1, :])
+    hop = Team(p, vecs, team, team_s.at[0], team_r.at[0])
+    reduce = Reduce(p, stage, (rc, rx, ry, rz, own, rf), fin, RJOBS, s_r, r_r)
+
+    def expand_tiles(start):
+        def body(n, carry):
+            cols = pl.ds(pl.multiple_of(start + n * 256, 256), 256)
+            stage[:, :, cols] = dot(n2t[...], dd[:, cols]).astype(B16).reshape(8, 96, 256)
+            return carry
+        lax.fori_loop(0, 3, body, 0)
+
+    text = jnp.concatenate([jnp.concatenate([texts[i, :, r, :] for r in range(4)], 1) for i in range(4)], 0)
     text_unit = (text * lax.rsqrt(jnp.sum(text * text, -1, keepdims=True) + 1e-06)).astype(B16)
+    loads[0].wait()
+    loads[1].wait()
     hop.wait()
     total = team[0] + team[1] + team[2] + team[3]
-    hop.done()
     for k in range(8):
         gs[k] = jnp.broadcast_to(total[k : k + 1, 0:384], (8, 384))
+    hop.done()
     hop = Spread(p, gs, gr, hop_s.at[0], hop_r.at[0])
+    expand_tiles(0)
+    reduce.next(0)
     hop.wait()
     gated = jnp.concatenate([gr[v][0:1] for v in range(8)], 0)
     both = dot(twice(gated), shrink[...])
@@ -541,16 +583,17 @@
         ps[v] = pack_row(part[v : v + 1])
     hop.done()
     hop = Spread(p, ps, pr, hop_s.at[1], hop_r.at[1])
+    expand_tiles(D)
+    reduce.next(1, 0)
     hop.wait()
     packed = total[:, 384:512]
     for k in range(8):
         packed = packed + pr[k]
     hop.done()
-    load.wait()
+    loads[2].wait()
     denominator = (counts[0] * 197).astype(F32)
     pooled = jnp.broadcast_to(unpack_row(packed / denominator), (8, D))
-    pooled_low = pooled.astype(B16)
-    embed = dot(pooled_low, projection[...])
+    embed = dot(pooled.astype(B16), projection[...])
     rate = lax.rsqrt(jnp.sum(embed * embed, -1, keepdims=True) + 1e-06)
     unit = embed * rate
     logits = dot(unit.astype(B16), text_unit, 1, 1) * LOGIT_SCALE
@@ -562,12 +605,10 @@
     unit_grad = dot(slope, text_unit) * LOGIT_SCALE
     embed_grad = (rate * (unit_grad - unit * jnp.sum(unit * unit_grad, -1, keepdims=True))).astype(B16)
     rg = dot(embed_grad, projection[...], 1, 1) / denominator
-    rg_o[...] = rg
-    top = lax.broadcasted_iota(jnp.int32, (16, 1), 0) == 0
-    pooled_o[...] = jnp.where(top, jnp.concatenate([pooled, pooled], 0), 0.0).astype(B16)
-    eg_o[...] = jnp.where(top, jnp.concatenate([embed_grad.astype(F32)] * 2, 0), 0.0).astype(B16)
     rs_[...] = pack_row(rg.astype(B16).astype(F32)[0:1])
     hop = Spread(p, rs_, rr, hop_s.at[2], hop_r.at[2], same=True)
+    expand_tiles(2 * D)
+    reduce.next(2, 1)
     hop.wait()
     rows = jnp.concatenate([unpack_row(rr[v]) for v in range(8)], 0).astype(B16)
     grad = dot(rows, shrink[...], 1, 1)
@@ -575,49 +616,35 @@
         us[v] = jnp.broadcast_to(grad[v : v + 1], (8, 384))
     hop.done()
     hop = Spread(p, us, ur, hop_s.at[3], hop_r.at[3])
-    shrink_grad_o[...] = dot(twice(gated), jnp.concatenate([rows.astype(F32)] * 2, 0).astype(B16), 0, 0)
+    expand_tiles(3 * D)
+    reduce.next(3, 2)
     hop.wait()
     for k in range(8):
-        gg_o[:, 384 * k : 384 * k + 384] = ur[k]
+        gg[:, 384 * k : 384 * k + 384] = ur[k]
     hop.done()
 
-
-def backward_kernel(
-    xs, normt_h, mixed_h, shares, seen_h, seent_h, hidden_h, n2t_h, d_h, full, gg, rg, gains, mout, counts,
-    stage, patch_o, first_o, mog_o,
-    wexp, wmerge, wheads, normt, mixed, seen, seent, hidden, n2t, dd, sbuf, hg, low, dout, lsem, psem,
-):
-    p = Pos()
-    jobs = ((n2t_h, n2t), (d_h, dd), (full.at[:, pl.ds(EXPAND, 3072)], wexp), (hidden_h, hidden),
-            (seent_h, seent), (full.at[:, pl.ds(AMERGE, D)], wmerge), (mixed_h, mixed), (seen_h, seen), (normt_h, normt),
-            (full.at[:, pl.ds(AHEADS, 3 * D)], wheads))
-    loads = []
-    for index, (source, target) in enumerate(jobs):
-        copy = pltpu.make_async_copy(source, target, lsem.at[index])
-        copy.start()
-        loads.append(copy)
+    def scale_tile(n, carry):
+        cols = pl.ds(pl.multiple_of(n * 256, 256), 256)
+        dd[:, cols] = (dd[:, cols].astype(F32) * gg[0:1, cols]).astype(B16)
+        return carry
+
+    lax.fori_loop(0, 12, scale_tile, 0)
+    reduce.next(0, 3, scale=gg)
+    loads[3].wait()
+
+    def norm_tile(n):
+        hg[:, 256 * n : 256 * n + 256] = dot(dd[...], wx[256 * n : 256 * n + 256, :], 1, 1)
+
+    norm_tile(0)
+    reduce.next(1, scale=gg)
+    norm_tile(1)
+    reduce.next(0, 2, scale=gg)
+    norm_tile(2)
+    weights = [load(full.at[:, pl.ds(CHEADS, 3 * D)], wx.at[:, pl.ds(0, 3 * D)]), load(full.at[:, pl.ds(COURIER, D)], wx.at[:, pl.ds(3 * D, D)])]
+    shrink_grad_o[...] = dot(twice(gated), jnp.concatenate([rows.astype(F32)] * 2, 0).astype(B16), 0, 0)
+    reduce.next(1, 3, scale=gg)
+    loads[4].wait()
     attend_gain, expand_gain = gains[1:2, :], gains[2:3, :]
-    loads[0].wait()
-    loads[1].wait()
-
-    def expand_tile(n, carry):
-        cols = pl.ds(pl.multiple_of(n * 256, 256), 256)
-        tile = dd[:, cols]
-        scale = gg[0:1, cols]
-        stage[:, :, cols] = (dot(n2t[...], tile) * scale).astype(B16).reshape(8, 96, 256)
-        dd[:, cols] = (tile.astype(F32) * scale).astype(B16)
-        return carry
-
-    lax.fori_loop(0, 12, expand_tile, 0)
-    loads[2].wait()
-
-    def norm_tile(n, carry):
-        cols = pl.ds(pl.multiple_of(n * 256, 256), 256)
-        hg[:, cols] = dot(dd[...], wexp[cols, :], 1, 1)
-        return carry
-
-    lax.fori_loop(0, 3, norm_tile, 0)
-    loads[3].wait()
 
     def hidden_frame(f, total):
         here = pl.ds(pl.multiple_of(f * PAD, 16), PAD)
@@ -633,8 +660,9 @@
         return total + jnp.sum(dy * xh, 0, keepdims=True)
 
     expand_gain_grad = lax.fori_loop(0, 4, hidden_frame, jnp.zeros((1, D), F32))
-    loads[4].wait()
+    reduce.next(0, 2)
     loads[5].wait()
+    loads[6].wait()
 
     def merge_tile(n, carry):
         cols = pl.ds(pl.multiple_of(n * 256, 256), 256)
@@ -643,56 +671,76 @@
         return carry
 
     lax.fori_loop(0, 3, merge_tile, 0)
-    loads[6].wait()
+    weights.append(load(full.at[:, pl.ds(CMERGE, D)], wmerge))
+    reduce.next(4, 1, 3)
     loads[7].wait()
-    first = lax.broadcasted_iota(jnp.int32, (PAD, 128), 1) < HEAD
+    loads[8].wait()
+    half_lanes = lax.broadcasted_iota(jnp.int32, (PAD, 128), 1) < HEAD
 
     def fetch(index, slot):
         return pltpu.make_async_copy(shares.at[pl.ds(index * 2, 2)], sbuf.at[slot], psem.at[slot])
 
     fetch(0, 0).start()
 
-    def attend(index, carry):
-        f, pair = index // 6, lax.rem(index, 6)
-        slot = lax.rem(index, 2)
-
-        @pl.when(index < 23)
-        def _():
-            fetch(index + 1, 1 - slot).start()
-
-        fetch(index, slot).wait()
-        here = pl.ds(pl.multiple_of(f * PAD, 16), PAD)
-        at = pl.multiple_of(pair * 128, 128)
-        qs, ks, vs = (pl.ds(pl.multiple_of(b + at, 128), 128) for b in (0, D, 2 * D))
-        q, k, v = mixed[here, qs], mixed[here, ks], mixed[here, vs]
-        do, o = dout[here, qs], seen[here, qs]
-        right = jnp.concatenate([do, (-(do.astype(F32) * o.astype(F32))).astype(B16)], 1)
-        dq = dk = dv = None
-        zero = jnp.zeros_like(q)
-        for h in range(2):
-            mask = first if h == 0 else jnp.logical_not(first)
-            share = sbuf[slot, h]
-            left = jnp.concatenate([jnp.where(mask, v, zero), jnp.where(mask, jnp.ones_like(v), zero)], 1)
-            ds = (share.astype(F32) * dot(left, right, 1, 1)).astype(B16)
-            pq = dot(ds, jnp.where(mask, k, zero), 0, 0)
-            pk = dot(ds, jnp.where(mask, q, zero))
-            pv = dot(share, jnp.where(mask, do, zero))
-            dq, dk, dv = (pq, pk, pv) if h == 0 else (dq + pq, dk + pk, dv + pv)
-        mixed[here, qs] = (dq * HEAD ** (-0.5)).astype(B16)
-        mixed[here, ks] = dk.astype(B16)
-        mixed[here, vs] = dv.astype(B16)
-        return carry
-
-    lax.fori_loop(0, 24, attend, 0)
-    loads[8].wait()
-
-    def heads_tile(n, carry):
-        cols = pl.ds(pl.multiple_of(n * 256, 256), 256)
-        stage[:, :, pl.ds(pl.multiple_of(3840 + n * 256, 128), 256)] = dot(normt[...], mixed[:, cols]).astype(B16).reshape(8, 96, 256)
-        return carry
-
-    lax.fori_loop(0, 9, heads_tile, 0)
+    def attend_frame(f):
+        def attend(pair, carry):
+            index = f * 6 + pair
+            slot = lax.rem(index, 2)
+
+            @pl.when(index < 23)
+            def _():
+                fetch(index + 1, 1 - slot).start()
+
+            fetch(index, slot).wait()
+            here = pl.ds(f * PAD, PAD)
+            at = pl.multiple_of(pair * 128, 128)
+            qs, ks, vs = (pl.ds(pl.multiple_of(b + at, 128), 128) for b in (0, D, 2 * D))
+            q, k, v = mixed[here, qs], mixed[here, ks], mixed[here, vs]
+            do, o = dout[here, qs], seen[here, qs]
+            right = jnp.concatenate([do, (-(do.astype(F32) * o.astype(F32))).astype(B16)], 1)
+            dq = dk = dv = None
+            zero = jnp.zeros_like(q)
+            for h in range(2):
+                mask = half_lanes if h == 0 else jnp.logical_not(half_lanes)
+                share = sbuf[slot, h]
+                left = jnp.concatenate([jnp.where(mask, v, zero), jnp.where(mask, jnp.ones_like(v), zero)], 1)
+                ds = (share.astype(F32) * dot(left, right, 1, 1)).astype(B16)
+                pq = dot(ds, jnp.where(mask, k, zero), 0, 0)
+                pk = dot(ds, jnp.where(mask, q, zero))
+                pv = dot(share, jnp.where(mask, do, zero))
+                dq, dk, dv = (pq, pk, pv) if h == 0 else (dq + pq, dk + pk, dv + pv)
+            mixed[here, qs] = (dq * HEAD ** (-0.5)).astype(B16)
+            mixed[here, ks] = dk.astype(B16)
+            mixed[here, vs] = dv.astype(B16)
+            return carry
+        lax.fori_loop(0, 6, attend, 0)
+
+    attend_frame(0)
+    reduce.next(4, 2, 0)
+    attend_frame(1)
+    reduce.next(3, 1)
+    attend_frame(2)
+    reduce.next(4, 2, 0, 0)
+    attend_frame(3)
+    tokens = load(xs_h, dout)
+    reduce.next(4, 3, 1)
     loads[9].wait()
+
+    def heads_tiles(start):
+        def body(n, carry):
+            cols = pl.ds(pl.multiple_of(start + n * 256, 256), 256)
+            to = pl.ds(pl.multiple_of(3840 + start + n * 256, 128), 256)
+            stage[:, :, to] = dot(normt[...], mixed[:, cols]).astype(B16).reshape(8, 96, 256)
+            return carry
+        lax.fori_loop(0, 3, body, 0)
+
+    heads_tiles(0)
+    reduce.next(5, 4)
+    heads_tiles(D)
+    reduce.next(5, 6, 2, 3)
+    heads_tiles(2 * D)
+    reduce.next(6, 7, 4)
+    loads[10].wait()
 
     def tokens_tile(n, carry):
         cols = pl.ds(pl.multiple_of(n * 256, 256), 256)
@@ -700,58 +748,40 @@
         return carry
 
     lax.fori_loop(0, 3, tokens_tile, 0)
-    attend_gain_grad = jnp.zeros((1, D), F32)
-    firsts, messages = [], []
+    reduce.next(5, 7)
+    tokens.wait()
     spot = lax.broadcasted_iota(jnp.int32, (PAD, 1), 0) == 197
-    for f in range(4):
-        here = pl.ds(f * PAD, PAD)
-        xh, rate = normalize(jnp.where(spot, mout[f : f + 1, :], xs[f].astype(F32)))
+    place = lax.broadcasted_iota(jnp.int32, (8, D), 0)
+    first[...] = jnp.zeros_like(first)
+    mog[...] = jnp.zeros_like(mog)
+
+    def token_frame(f, total):
+        here = pl.ds(pl.multiple_of(f * PAD, 16), PAD)
+        xh, rate = normalize(jnp.where(spot, row_of(mout[...], f), dout[here, :].astype(F32)))
         dy = hidden[here, :]
         e = dy * attend_gain
         grad = rate * (e - jnp.mean(e, -1, keepdims=True) - xh * jnp.mean(e * xh, -1, keepdims=True))
-        attend_gain_grad = attend_gain_grad + jnp.sum(dy * xh, 0, keepdims=True)
         patch = hg[here, :] + grad
-        patch_o[f] = patch.astype(B16)
-        firsts.append(patch[0:1])
-        messages.append(grad[197:198])
-    first_o[...] = jnp.concatenate(firsts + [jnp.zeros((4, D), F32)], 0)
-    mog_o[...] = jnp.concatenate(messages + [jnp.zeros((4, D), F32)], 0)
+        low[here, :] = patch.astype(B16)
+        first[...] = jnp.where(place == f, patch[0:1], first[...])
+        mog[...] = jnp.where(place == f, grad[197:198], mog[...])
+        return total + jnp.sum(dy * xh, 0, keepdims=True)
+
+    attend_gain_grad = lax.fori_loop(0, 4, token_frame, jnp.zeros((1, D), F32))
+    hop = Team(p, mog, mog_team, team_s.at[1], team_r.at[1])
+    patch_out = load(low, patch_h)
+    reduce.next(6, 5)
     tall = jnp.concatenate([attend_gain_grad, expand_gain_grad, jnp.zeros((126, D), F32)], 0)
     stage[:, :, 6144:6272] = jnp.transpose(tall).astype(B16).reshape(8, 96, 128)
-
-
-RJOBS = ((0, 768), (768, 768), (1536, 768), (2304, 768), (3072, 768), (3840, 768), (4608, 768), (5376, 896))
-BUNDLE = 8448
-SIXTH = BUNDLE // 6
-
-
-def reduce_kernel(
-    stage_h, mog, first, full, leaders, message, mnorm, mmix, mshare, told, pooled, eg, gains,
-    out, courier_o, cheads_o, cmerge_o, proj_o, cgain_o, lead_o,
-    stage, rc, rx, ry, rz, own, rf, fin, rcf, bundle, team, weights, s_r, r_r, s_b, r_b, team_s, team_r, lsem,
-):
-    p = Pos()
-    loads = []
-    for index, (first_col, count, target) in enumerate(((CMERGE, D, 3072), (CHEADS, 3 * D, D), (COURIER, D, 0))):
-        loads.append(pltpu.make_async_copy(full.at[:, pl.ds(first_col, count)], weights.at[:, pl.ds(target, count)], lsem.at[index]))
-        loads[-1].start()
-    big = pltpu.make_async_copy(stage_h, stage, lsem.at[3])
-    big.start()
-    barrier(p.peers() + [p.cross])
-    hop = Team(p, mog, team, team_s, team_r)
-    big.wait()
-    reduce = Reduce(p, stage, (rc, rx, ry, rz, own, rf, fin, rcf), out, RJOBS, s_r, r_r)
-    lag = (0, 1, 2, 3, 4, 5, 6, 7)
-    reduce.tick(0, lag)
-    reduce.tick(1, lag)
+    reduce.next(8, 4)
+    for copy in weights:
+        copy.wait()
     hop.wait()
-    out_grad = jnp.concatenate([team[i][0:4] for i in range(4)], 0)
-    for load in loads:
-        load.wait()
+    out_grad = jnp.concatenate([mog_team[i][0:4] for i in range(4)], 0)
     courier_gain = gains[0:1, :]
     mq, mk, mv = mmix[:, 0:D], mmix[:, D : 2 * D], mmix[:, 2 * D : 3 * D]
     out_low = out_grad.astype(B16)
-    told_grad = dot(out_low, weights[:, 3072:3840], 1, 1).astype(B16)
+    told_grad = dot(out_low, wmerge[...], 1, 1).astype(B16)
     upstream = spread_heads(told_grad)
     share = mshare[...]
     share_grad = dot(upstream, mv, 1, 1)
@@ -761,14 +791,15 @@
     dq = join_heads(dot(ds, mk)) * HEAD ** (-0.5)
     dk = dot(ds, spread_heads(mq), 0, 0) * HEAD ** (-0.5)
     mixed_grad = jnp.concatenate([dq, dk, dv], 1).astype(B16)
-    norm_grad = dot(mixed_grad, weights[:, D : 4 * D], 1, 1)
+    norm_grad = dot(mixed_grad, wx[:, 0 : 3 * D], 1, 1)
     xh, rate = normalize(message[...])
     e = norm_grad * courier_gain
     grad = rate * (e - jnp.mean(e, -1, keepdims=True) - xh * jnp.mean(e * xh, -1, keepdims=True))
     message_grad = (out_grad + grad).astype(B16)
-    leader_grad = dot(message_grad, weights[:, 0:D], 1, 1)
-    lead_o[...] = jnp.concatenate([row_of(leader_grad, p.dp * 4 + f) for f in range(4)] + [jnp.zeros((4, D), F32)], 0) + first[...]
-    parts = (message_grad, mixed_grad, out_low, leaders[...], mnorm[...], told[...], pooled[...], eg[...],
+    top = lax.broadcasted_iota(jnp.int32, (16, 1), 0) == 0
+    pooled_rows = jnp.where(top, jnp.concatenate([pooled, pooled], 0), 0.0).astype(B16)
+    embed_rows = jnp.where(top, jnp.concatenate([embed_grad.astype(F32)] * 2, 0), 0.0).astype(B16)
+    parts = (message_grad, mixed_grad, out_low, leaders[...], mnorm[...], told[...], pooled_rows, embed_rows,
              (norm_grad * xh).astype(B16))
     col = 0
     for part in parts:
@@ -779,9 +810,17 @@
         return bundle.at[k, :, pl.ds(pl.multiple_of(start * SIXTH, 128), count * SIXTH)]
 
     gather = Gather(p, block, 1, s_b, r_b)
-    for t in range(2, 8):
-        gather.stage(t - 2, 0)
-        reduce.tick(t, lag)
+    gather.stage(0, 0)
+    leader_grad = dot(message_grad, wx[:, 3 * D : 4 * D], 1, 1)
+    lead_o[...] = jnp.concatenate([row_of(leader_grad, p.dp * 4 + f) for f in range(4)] + [jnp.zeros((4, D), F32)], 0) + first[...]
+    reduce.next(7, 6, 8)
+    gather.stage(1, 0)
+    reduce.next(5)
+    gather.stage(2, 0)
+    reduce.next(7, 6, 8)
+    gather.stage(3, 0)
+    reduce.next(5, 8)
+    gather.stage(4, 0)
     whole = bundle[...].reshape(128, BUNDLE)
     pick = jnp.where(
         jnp.logical_and(lax.broadcasted_iota(jnp.int32, (D, 128), 0) == p.k * 96 + lax.broadcasted_iota(jnp.int32, (D, 128), 1),
@@ -793,15 +832,25 @@
 
     courier_o[...] = product(3840, D, 0, D)
     cheads_o[...] = product(4608, D, D, 3 * D)
+    reduce.next(7, 6, 8)
     cmerge_o[...] = product(5376, D, 3072, D)
     proj_o[...] = product(6144, D, 6912, 512)
     gain_grad = jnp.sum(whole[:, 7424:8192].astype(F32), 0, keepdims=True)
     gain_grad = twice(jnp.broadcast_to(gain_grad, (8, D)))
     both = dot(pick, gain_grad, 0, 1)
     cgain_o[...] = both[0:96, 0:8] + both[0:96, 8:16]
-    for t in range(8, len(RJOBS) + 7):
-        reduce.tick(t, lag)
+    for _ in range(8):
+        for job in range(len(RJOBS)):
+            if reduce.at[job] < 7:
+                reduce.next(job)
+    for job in range(len(RJOBS)):
+        reduce.next(job)
+    gather.stage(5, 0)
     hop.done()
+    patch_out.wait()
+
+
+VMEM = 62 * 1024 * 1000
 
 
 def any_spec():
@@ -856,46 +905,30 @@
         compiler_params=pltpu.CompilerParams(collective_id=0, has_side_effects=True, vmem_limit_bytes=60 << 20),
         name="forward",
     )(xs, lead, caption, counts, courier, gain_block, courier_heads, attend_heads, courier_merge, attend_merge, expand_weight, projection)
-    gg, rg, loss, shrink_grad, pooled, eg = pl.pallas_call(
-        loss_kernel,
-        out_shape=(sds((8, 4 * D), F32), sds((8, D), F32), sds((8, 128), F32), sds((384, D), F32), sds((16, D), B16),
-                   sds((16, 512), B16)),
-        in_specs=[vmem, vmem, vmem, anys, vmem, smem, smem],
-        out_specs=tuple([vmem] * 6),
+    (patch, fin, loss, shrink_grad, courier_grad, cheads_grad, cmerge_grad, proj_grad, cgain, leads) = pl.pallas_call(
+        rear_kernel,
+        out_shape=(
+            sds((ROWS, D), B16), sds((96, 6272), B16), sds((8, 128), F32), sds((384, D), F32), sds((96, D), F32),
+            sds((96, 3 * D), F32), sds((96, D), F32), sds((96, 512), F32), sds((96, 8), F32), sds((8, D), F32)),
+        in_specs=[anys] * 10 + [vmem] * 12 + [smem] * 2,
+        out_specs=tuple([anys] + [vmem] * 9),
         scratch_shapes=[
+            vm((8, 96, 6272), B16), vm((4, 8, 48, D), B16), vm((8, 16, 6272), B16), vm((4, 32, 6272), B16),
+            vm((3, 32, 6272), B16), vm((32, 6272), B16), vm((32, 6272), B16), vm((8, 16, BUNDLE), B16),
+            vm((D, 4 * D), B16), vm((D, D), B16), vm((D, 3 * D), B16), vm((D, ROWS), B16), vm((ROWS, 3 * D), B16),
+            vm((ROWS, D), B16), vm((D, ROWS), B16), vm((ROWS, D), F32), vm((D, ROWS), B16), vm((ROWS, 4 * D), B16),
+            vm((2, 2, PAD, PAD), B16), vm((ROWS, D), F32), vm((ROWS, D), B16), vm((ROWS, D), B16),
             vm((D, 512), B16), vm((8, 512), F32), vm((4, 8, 512), F32), vm((8, 8, 384), F32), vm((8, 8, 384), F32),
             vm((8, 8, 128), F32), vm((8, 8, 128), F32), vm((8, 128), F32), vm((8, 8, 128), F32), vm((8, 8, 384), F32),
-            vm((8, 8, 384), F32), dma(3), dma(3), dma(4, 7), dma(4, 7), pltpu.SemaphoreType.DMA],
-        compiler_params=pltpu.CompilerParams(collective_id=1, has_side_effects=True, vmem_limit_bytes=60 << 20),
-        name="loss",
-    )(gsum, hsum, shrink_weight, full, texts, counts, matches)
-    stage, patch, first, mog = pl.pallas_call(
-        backward_kernel,
-        out_shape=(sds((8, 96, 6272), B16), sds((4, PAD, D), B16), sds((8, D), F32), sds((8, D), F32)),
-        in_specs=[vmem, anys, anys, anys, anys, anys, anys, anys, anys, anys, vmem, vmem, vmem, vmem, smem],
-        out_specs=tuple([vmem] * 4),
-        scratch_shapes=[
-            vm((D, 4 * D), B16), vm((D, D), B16), vm((D, 3 * D), B16), vm((D, ROWS), B16), vm((ROWS, 3 * D), B16),
-            vm((ROWS, D), B16), vm((D, ROWS), B16), vm((ROWS, D), F32), vm((D, ROWS), B16), vm((ROWS, 4 * D), B16),
-            vm((2, 2, PAD, PAD), B16), vm((ROWS, D), F32), vm((ROWS, D), B16), vm((ROWS, D), B16), dma(10), dma(2)],
-        compiler_params=pltpu.CompilerParams(vmem_limit_bytes=60 << 20),
-        name="backward",
-    )(xs, normt, mixed, shares, seen, seent, hidden, n2t, dd, full, gg, rg, gains, mout, counts)
-    out, courier_grad, cheads_grad, cmerge_grad, proj_grad, cgain, leads = pl.pallas_call(
-        reduce_kernel,
-        out_shape=(sds((96, 6272), F32), sds((96, D), F32), sds((96, 3 * D), F32), sds((96, D), F32), sds((96, 512), F32),
-                   sds((96, 8), F32), sds((8, D), F32)),
-        in_specs=[anys, vmem, vmem, anys] + [vmem] * 9,
-        out_specs=tuple([vmem] * 7),
-        scratch_shapes=[
-            vm((8, 96, 6272), B16), vm((8, 48, 6272), B16), vm((8, 16, 6272), B16), vm((4, 32, 6272), B16),
-            vm((3, 32, 6272), B16), vm((32, 6272), B16), vm((32, 6272), B16), vm((96, 6272), B16), vm((48, 6272), B16),
-            vm((8, 16, BUNDLE), B16), vm((4, 8, D), F32), vm((D, 5 * D), B16),
-            dma(len(RJOBS), 11), dma(len(RJOBS), 11), dma(1, 28), dma(1, 28), dma(3), dma(3), dma(4)],
-        compiler_params=pltpu.CompilerParams(collective_id=2, has_side_effects=True, vmem_limit_bytes=60 << 20),
-        name="reduce",
-    )(stage, mog, first, full, leaders, message, mnorm, mmix, mshare, told, pooled, eg, gains)
-    patch_grad = jnp.concatenate([leads[0:4, None, :].astype(B16), patch[:, 1:197]], 1)[None]
+            vm((8, 8, 384), F32), vm((8, 4 * D), F32), vm((8, D), F32), vm((8, D), F32), vm((4, 8, D), F32),
+            dma(len(RJOBS), 11), dma(len(RJOBS), 11), dma(1, 28), dma(1, 28), dma(2, 3), dma(2, 3), dma(4, 7), dma(4, 7),
+            dma(16), dma(2)],
+        compiler_params=pltpu.CompilerParams(collective_id=1, has_side_effects=True, vmem_limit_bytes=VMEM),
+        name="rear",
+    )(xs.reshape(ROWS, D), normt, mixed, shares, seen, seent, hidden, n2t, dd, full, gsum, hsum, shrink_weight, texts, gains, mout,
+      leaders, message, mnorm, mmix, mshare, told, counts, matches)
+    patch_grad = jnp.concatenate([leads[0:4, None, :].astype(B16), patch.reshape(4, PAD, D)[:, 1:197]], 1)[None]
+    out = fin.astype(F32)
     return (
         loss[0:1, 0], patch_grad, courier_grad, cgain[:, 0], cheads_grad, cmerge_grad, out[:, 6144], out[:, 3840:6144],
         out[:, 3072:3840], out[:, 6145], out[:, 0:3072], shrink_grad, proj_grad,

time: 300 us -> 262 us (0.87)
  Pallas kernels: 278 us -> 237 us
  other arithmetic: 1.54 us -> 4.57 us
    pallas_call x3 -> x1, Pallas kernels: 166 us -> 125 us  [fast(): pl.pallas_call(rear_kernel, out_shape=(sds((ROWS, D), B16), sds((96, 6272...]
    unnamed x29 -> x23, local copies, waits for them, and re-layouts: 7.7 us -> 6.66 us
where the time goes in v2:
time: 262 us; the launch traced here: 261 us
  Pallas kernels  237 us (90%)
  local copies, waits for them, and re-layouts  17.1 us (7%)
  other arithmetic  4.57 us (2%)
    pallas_call x1, Pallas kernels, fast(): pl.pallas_call(rear_kernel, out_shape=(sds((ROWS, D), B16), sds((96, 6272...  125 us
    pallas_call x1, Pallas kernels, fast(): pl.pallas_call(forward_kernel, out_shape=(sds((D, NCOLS), B16), sds((D, R...  112 us
    unnamed x23, local copies, waits for them, and re-layouts  6.66 us

profile of v2, /device:TPU:0, one launch (start us, length us, event | category | flops | bytes accessed | tf_op | source)
XLA Modules:
  0.0 260.8 jit_solution(2358263955181770566)
XLA Ops:
  1.9 0.7 reduce
  2.6 0.7 pad_maximum_fusion
  3.3 0.6 pad_convert_fusion.1.caption
  3.9 0.7 slice_bitcast_fusion
  4.6 0.6 pad_convert_fusion.lead
  5.2 0.1 copy.39
  5.4 0.6 pad.25.gains
  6.0 1.4 copy.43
  7.4 1.2 pad.20.xs
  8.6 111.9 %forward.1 = (bf16[768,10624]{1,0:T(8,128)(2,1)}, bf16[768,832]{1,0:T(8,128)(2,1)}, bf16[832,2304]{1,0:T(8,128)(2,1)}, bf16[48,208,208]{2,1,0:T(8,128)(2,1)}, bf...) custom-call(bf16[4,208,768]{2,1,0:T(8,128)(2,1)} %pad.20.xs, ...), custom_call_target="tpu_custom_call" | custom-call | tf_op jit(solution)/shard_map/forward/pallas_call | solution.py:891
  120.4 125.4 %rear.1 = (bf16[832,768]{1,0:T(8,128)(2,1)}, bf16[96,6272]{1,0:T(8,128)(2,1)}, f32[8,128]{1,0:T(8,128)}, f32[384,768]{1,0:T(8,128)}, f32[96,768]{1,0:T(8,128)}, ...) custom-call(bf16[832,768]{1,0:T(8,128)(2,1)} %bitcast.16, ...), custom_call_target="tpu_custom_call" | custom-call | tf_op jit(solution)/shard_map/rear/pallas_call | solution.py:908
  245.8 0.0 copy-start
  245.8 1.3 slice.32
  247.1 0.7 fusion
  247.8 1.6 slice.45
  249.5 2.0 slice.44
  251.4 0.0 copy-done
  251.5 1.1 slice.47
  252.6 0.0 copy-start.7
  252.6 0.0 copy-start.1
  252.6 0.2 convert_element_type.22
  252.7 0.6 copy-done.7
  253.4 0.7 slice_reduce_fusion
  254.1 0.0 copy-done.1
  254.1 0.3 slice.42
  254.4 0.5 copy.41
  254.9 0.0 copy-start.5
  254.9 0.0 copy-start.3
  254.9 1.8 maximum_bitcast_fusion
  256.7 0.0 copy-done.5
  256.7 0.0 copy-start.4
  256.7 0.7 copy.51
  257.4 0.0 copy-done.3
  257.4 0.0 copy-start.2
  257.4 0.9 copy.52
  258.3 0.0 copy-done.4
  258.3 0.7 copy.53
  259.0 0.0 copy-done.2
  259.1 0.0 copy-start.6
  259.1 1.0 copy.54
  260.1 0.1 copy-done.6
  260.2 0.7 copy.55
Async XLA Ops:
  245.8 5.7 %copy-start = (bf16[96,6272]{1,0:T(8,128)(2,1)S(1)}, bf16[96,6272]{1,0:T(8,128)(2,1)}, u32[]{:S(2)}) copy-start(bf16[96,6272]{1,0:T(8,128)(2,1)} %get-tuple-element.70) | copy-start | bytes 3612676
  252.6 0.8 copy-start.7
  252.6 1.5 copy-start.1
  254.9 1.8 copy-start.5
  254.9 2.5 copy-start.3
  256.7 1.6 copy-start.4
  257.4 1.6 copy-start.2
  259.1 1.1 copy-start.6
